TPU v7x, 256 devices: a whole 4x4x8 slice. The times are simulated.
256 devices in a mesh: dp: 32 (over y, x, core), mp: 8 (over z).
Axes of the slice: x: 4, y: 4, z: 8, core: 2. Of those that a mesh axis runs over, the one named last changes fastest.
Arguments:
- tokens: bfloat16 [2048, 7168], P('dp', 'mp'), may hold values from -6 to 6
- expert_ids: int32 [2048, 8], P('dp'), may hold values from 0 to 31, all different within a row; in each aligned block of 64 rows (0 to 63, 64 to 127, ...) at most 24 rows name the same one
- route_weights: float32 [2048, 8], P('dp'), may hold values from 0.2 to 1
- placement_of: int32 [32], replicated, may hold values from 0 to 31, each once
- gate_weight: bfloat16 [32, 7168, 1024], P(None, 'dp', 'mp'), may hold values from -0.0625 to 0.0625
- up_weight: bfloat16 [32, 7168, 1024], P(None, 'dp', 'mp'), may hold values from -0.0625 to 0.0625
- down_weight: bfloat16 [32, 7168, 1024], P(None, 'dp', 'mp'), may hold values from -0.1875 to 0.1875
Outputs:
- rollout_gate: bfloat16 [32, 7168, 1024], P('dp', None, 'mp')
- rollout_up: bfloat16 [32, 7168, 1024], P('dp', None, 'mp')
- rollout_down: bfloat16 [32, 7168, 1024], P('dp', None, 'mp')
- rollout_scales: float32 [3, 32, 56, 8], P(None, 'dp', None, 'mp')
- mixed: bfloat16 [2048, 7168], P('dp', 'mp')
Inputs may be any that keep to these rules, and one draw needn't show every extreme that they name: `expert_ids`: each row names 8 different experts. In each aligned block of 64 rows (the tokens of one index of dp) no expert is named by more than 24 rows, a bound that some block reaches. `placement_of`: A permutation; slot s is held by the owner of dp index s.
All inputs are finite; a program needn't handle non-finite values. Where the computation divides by a largest or mean magnitude, that divisor is 1e-20 or more.
Results may differ from a plain program's by a relative error of at most 0.02.
Values may be sent and summed in bfloat16 or wider, within the bound.
A program may use at most 192 MiB of HBM per device.

v0:
```python
import jax
import jax.numpy as jnp
from jax import lax
from jax.sharding import PartitionSpec as P

D = 7168
BLK = 128
CAP = 24


EPS = 1e-06


def quantize_local(matrices):
    count, rows, cols = matrices.shape
    blocks = matrices.astype(jnp.float32).reshape(count, rows // BLK, BLK, cols // BLK, BLK)
    scale = jnp.max(jnp.abs(blocks), axis=(2, 4)) + EPS
    quant = (blocks / scale[:, :, None, :, None]).astype(jnp.bfloat16).reshape(count, rows, cols)
    return (quant, scale)


def local(tokens, expert_ids, route_weights, placement_of, gate_weight, up_weight, down_weight):
    dp_count = lax.axis_size("dp")
    experts = placement_of.shape[0]
    per_owner = experts // dp_count
    tok_rows, choices_per = expert_ids.shape
    inverse = jnp.argsort(placement_of)
    ordered = (
        jnp.take(gate_weight, inverse, axis=0),
        jnp.take(up_weight, inverse, axis=0),
        jnp.take(down_weight, inverse, axis=0),
    )
    got_gate, got_up, got_down = (
        lax.all_to_all(ordered[0], "dp", split_axis=0, concat_axis=1, tiled=True),
        lax.all_to_all(ordered[1], "dp", split_axis=0, concat_axis=1, tiled=True),
        lax.all_to_all(ordered[2], "dp", split_axis=0, concat_axis=1, tiled=True),
    )
    gate_q, gate_s = quantize_local(got_gate)
    up_q, up_s = quantize_local(got_up)
    down_q, down_s = quantize_local(got_down)
    flat = expert_ids.reshape(-1)
    hits = (flat[:, None] == jnp.arange(experts, dtype=jnp.int32)[None, :]).astype(jnp.int32)
    position = jnp.sum((jnp.cumsum(hits, axis=0) - hits) * hits, axis=1)
    target = jnp.take(placement_of, flat) * CAP + position
    token_of = jnp.arange(tok_rows * choices_per, dtype=jnp.int32) // choices_per
    row_token = jnp.full((experts * CAP,), tok_rows, jnp.int32).at[target].set(token_of)
    slot_rows = jnp.arange(experts * CAP, dtype=jnp.int32)
    combine = jnp.sum(
        jnp.where(
            target.reshape(tok_rows, choices_per)[:, :, None] == slot_rows[None, None, :],
            route_weights[:, :, None],
            0.0,
        ),
        axis=1,
    )
    whole = lax.all_gather(tokens, "mp", axis=1, tiled=True)
    padded = jnp.concatenate([whole, jnp.zeros((1, D), jnp.bfloat16)], axis=0)
    outgoing = padded[row_token].reshape(dp_count, per_owner * CAP, D)
    arrived = lax.all_to_all(outgoing, "dp", split_axis=0, concat_axis=0, tiled=True)
    arrived = arrived.reshape(dp_count, per_owner, CAP, D // BLK, BLK)
    groups = gate_q.shape[2] // BLK

    def project(quant, scale):
        per_block = jnp.einsum(
            "seckb,ekbgf->seckgf",
            arrived,
            quant.reshape(per_owner, D // BLK, BLK, groups, BLK),
            preferred_element_type=jnp.float32,
        )
        return jnp.einsum("seckgf,ekg->secgf", per_block, scale, precision=lax.Precision.HIGHEST)

    gate = project(gate_q, gate_s)
    up = project(up_q, up_s)
    hidden = (jax.nn.silu(gate) * up).astype(jnp.bfloat16)
    per_block = jnp.einsum(
        "secgf,ekbgf->seckgb",
        hidden,
        down_q.reshape(per_owner, D // BLK, BLK, groups, BLK),
        preferred_element_type=jnp.float32,
    )
    partial_value = (
        jnp.einsum("seckgb,ekg->seckb", per_block, down_s, precision=lax.Precision.HIGHEST)
        .astype(jnp.bfloat16)
        .reshape(dp_count, per_owner, CAP, D)
    )
    sums = lax.psum_scatter(
        partial_value.astype(jnp.float32).astype(jnp.bfloat16),
        "mp",
        scatter_dimension=3,
        tiled=True,
    ).astype(jnp.float32)
    back = (
        lax.all_to_all(sums.astype(jnp.bfloat16), "dp", split_axis=0, concat_axis=0, tiled=True)
        .astype(sums.dtype)
        .reshape(experts * CAP, -1)
    )
    mixed = jnp.dot(combine, back, precision=lax.Precision.HIGHEST)
    scales = jnp.stack([gate_s, up_s, down_s])
    return (gate_q, up_q, down_q, scales, mixed.astype(jnp.bfloat16))


def solution(mesh):
    placed = (
        P("dp", "mp"),
        P("dp", None),
        P("dp", None),
        P(),
        P(None, "dp", "mp"),
        P(None, "dp", "mp"),
        P(None, "dp", "mp"),
    )
    return jax.shard_map(
        local,
        mesh=mesh,
        in_specs=placed,
        out_specs=(
            P("dp", None, "mp"),
            P("dp", None, "mp"),
            P("dp", None, "mp"),
            P(None, "dp", None, "mp"),
            P("dp", "mp"),
        ),
        check_vma=False,
    )
```

profile of v0, /device:TPU:10, one launch (start us, length us, event | category | flops | bytes accessed | tf_op | source)
XLA Modules:
  0.0 693.3 jit_solution(5149237376124689071)
XLA Ops:
  17.3 5.0 broadcast_select_fusion
  22.3 30.1 %all_to_all.37 = bf16[32,224,128]{2,1,0:T(8,128)(2,1)} all-to-all(bf16[32,224,128]{2,1,0:T(8,128)(2,1)S(1)} %get-tuple-element.73), channel_id=1, replica_groups=mesh['dp'=32,'mp'=8] {'dp'}, dimensions={0} | all-to-all | bytes 3670016 | tf_op jit(solution)/shard_map/all_to_all | solution.py:36
  52.3 7.2 %all-to-all-start.1 = ((bf16[32,224,128]{2,1,0:T(8,128)(2,1)}), bf16[32,224,128]{2,1,0:T(8,128)(2,1)S(1)}, u32[]{:S(2)}, u32[]{:S(2)}) async-start(bf16[32,224,128]{2,1,0:T(8,128)(2,1)} %get-tuple-element.74), calls=%async_computation.1 | async-start | bytes 3670016 | tf_op jit(solution)/shard_map/all_to_all | solution.py:35
  59.8 30.0 %all_gather.3 = bf16[64,7168]{1,0:T(8,128)(2,1)S(1)} all-gather(bf16[64,896]{1,0:T(8,128)(2,1)S(1)} %copy-done.9), channel_id=1, replica_groups=mesh['dp'=32,'mp'=8] {'mp'}, dimensions={1}, use_global_device_ids=true | all-gather | bytes 1032192 | tf_op jit(solution)/shard_map/all_gather | solution.py:56
  89.8 7.7 %all-to-all-start = ((bf16[32,224,128]{2,1,0:T(8,128)(2,1)}), bf16[32,224,128]{2,1,0:T(8,128)(2,1)}, u32[]{:S(2)}, u32[]{:S(2)}) async-start(bf16[32,224,128]{2,1,0:T(8,128)(2,1)} %get-tuple-element.75), calls=%async_computation | async-start | bytes 3670016 | tf_op jit(solution)/shard_map/all_to_all | solution.py:34
  100.8 4.3 compare_select_fusion.4
  105.3 15.8 %select_select_fusion = s32[512]{0:T(512)S(1)} fusion(pred[512]{0:T(512)(128)(4,1)S(1)} %get-tuple-element.32, pred[512]{0:T(512)(128)(4,1)S(1)} %get-tuple-element.30, pred[512]{0:T(512)(128)(4,1)S(1)} %get-tuple-element.31, pred[512]{0:T(512)(128)(4,1)S(1)} %get-tuple-element.29, pred[512]{0:T(512)(128)(4,1)S(1)} %get-tuple-element.28, ...), kind=kLoop, calls=%fused_computation.104 | loop fusion | flops 12800 | bytes 16996 | tf_op jit(solution)/shard_map/jit(_take)/gather | solution.py:44
  123.5 9.4 %gather_fusion = bf16[768,7168]{1,0:T(8,128)(2,1)} fusion(bf16[65,7168]{1,0:T(8,128)(2,1)S(1)} %concatenate.3, s32[1024]{0:T(1024)S(1)} %pad_clamp_fusion), kind=kCustom, calls=%fused_computation.3 | custom fusion | bytes 22023168 | tf_op jit(solution)/shard_map/gather | solution.py:58
  133.0 7.4 %all-to-all-start.3 = ((bf16[32,24,7168]{2,1,0:T(8,128)(2,1)}), bf16[32,24,7168]{2,1,0:T(8,128)(2,1)}, u32[]{:S(2)}, u32[]{:S(2)}) async-start(bf16[32,24,7168]{2,1,0:T(8,128)(2,1)} %bitcast.188), calls=%async_computation.3 | async-start | bytes 22020096 | tf_op jit(solution)/shard_map/all_to_all | solution.py:59
  156.2 114.5 %all-to-all-done.3 = bf16[32,24,7168]{2,1,0:T(8,128)(2,1)} async-done(((bf16[32,24,7168]{2,1,0:T(8,128)(2,1)}), bf16[32,24,7168]{2,1,0:T(8,128)(2,1)}, u32[]{:S(2)}, u32[]{:S(2)}) %all-to-all-start.3) | async-done | bytes 11010080 | tf_op jit(solution)/shard_map/all_to_all | solution.py:59
  270.7 10.4 %copy.81 = bf16[96,8,56,128]{3,2,1,0:T(8,128)(2,1)} copy(bf16[96,8,56,128]{3,1,2,0:T(8,128)(2,1)} %bitcast.99) | data formatting | bytes 22020096
  281.1 16.6 %fusion.13 = f32[32,24,56,128]{3,0,1,2:T(8,128)} fusion(bf16[32,24,56,128]{3,2,1,0:T(8,128)(2,1)} %bitcast.181, f32[56,128,128]{2,1,0:T(8,128)} %bitcast.186, f32[56]{0:T(128)S(1)} %get-tuple-element.76), kind=kOutput, calls=%fused_computation.17 | convolution fusion | flops 1411121152 | bytes 36700384 | tf_op jit(solution)/shard_map/seckb,ekbgf->seckgf/dot_general | solution.py:64
  297.7 29.0 %fusion.1 = f32[1,32,24,128]{3,0,2,1:T(1,128)S(1)} fusion(f32[32,24,56,128]{3,0,1,2:T(8,128)} %fusion.13, f32[56]{0:T(128)S(1)} %reduce_max.44), kind=kOutput, calls=%fused_computation.7 | convolution fusion | flops 66060344 | bytes 22413536 | tf_op jit(solution)/shard_map/seckgf,ekg->secgf/dot_general | solution.py:70
  326.8 16.6 %fusion.10 = f32[32,24,56,128]{3,0,1,2:T(8,128)} fusion(bf16[32,24,56,128]{3,2,1,0:T(8,128)(2,1)} %bitcast.182, f32[56,128,128]{2,1,0:T(8,128)} %bitcast.184, f32[56]{0:T(128)S(1)} %get-tuple-element.68), kind=kOutput, calls=%fused_computation.16 | convolution fusion | flops 1411121152 | bytes 36700384 | tf_op jit(solution)/shard_map/seckb,ekbgf->seckgf/dot_general | solution.py:64
  343.4 29.4 %fusion.3 = f32[1,32,24,128]{3,0,2,1:T(1,128)S(1)} fusion(f32[32,24,56,128]{3,0,1,2:T(8,128)} %fusion.10, f32[56]{0:T(128)S(1)} %reduce_max.38), kind=kOutput, calls=%fused_computation.9 | convolution fusion | flops 66060344 | bytes 22413536 | tf_op jit(solution)/shard_map/seckgf,ekg->secgf/dot_general | solution.py:70
  372.8 5.7 fusion.5
  378.5 53.0 %copy.78 = bf16[32,1,24,56,128]{2,0,4,3,1:T(8,128)(2,1)} copy(bf16[32,1,24,56,128]{4,0,2,3,1:T(8,128)(2,1)} %fusion.5) | data formatting | bytes 22020096
  431.4 81.1 %reshape.636 = bf16[7168,768]{1,0:T(8,128)(2,1)} reshape(bf16[7168,1,32,24]{3,2,1,0:T(8,128)(2,1)} %bitcast.183) | data formatting | bytes 22020096
  525.2 111.5 %reduce-scatter.4.cloned.1.call-done = bf16[896,768]{1,0:T(8,128)(2,1)} async-done(((bf16[7168,768]{1,0:T(8,128)(2,1)}), bf16[896,768]{1,0:T(8,128)(2,1)}) %reduce-scatter.4.cloned.1.call-update) | async-done | bytes 1376272
  636.7 13.4 %reshape.637 = bf16[896,1,32,24]{3,2,1,0:T(8,128)(2,1)} reshape(bf16[896,768]{1,0:T(8,128)(2,1)} %reduce-scatter.4.cloned.1.call-done) | data formatting | bytes 2752512
  650.1 9.8 %copy.77 = bf16[32,1,24,896]{3,2,0,1:T(8,128)(2,1)} copy(bf16[32,1,24,896]{2,0,1,3:T(8,128)(2,1)} %bitcast.189) | data formatting | bytes 2752512
  659.8 7.4 %all-to-all-start.4 = ((bf16[32,1,24,896]{3,2,1,0:T(8,128)(2,1)}), bf16[32,1,24,896]{3,2,1,0:T(8,128)(2,1)S(1)}, u32[]{:S(2)}, u32[]{:S(2)}) async-start(bf16[32,1,24,896]{3,2,1,0:T(8,128)(2,1)} %bitcast.193), calls=%async_computation.4 | async-start | bytes 2752512 | tf_op jit(solution)/shard_map/all_to_all | solution.py:93
  667.2 5.5 fusion.16
  672.8 12.1 %all-to-all-done.4 = bf16[32,1,24,896]{3,2,1,0:T(8,128)(2,1)S(1)} async-done(((bf16[32,1,24,896]{3,2,1,0:T(8,128)(2,1)}), bf16[32,1,24,896]{3,2,1,0:T(8,128)(2,1)S(1)}, u32[]{:S(2)}, u32[]{:S(2)}) %all-to-all-start.4) | async-done | bytes 1376288 | tf_op jit(solution)/shard_map/all_to_all | solution.py:93
  (87 shorter events, 45.9 us)
Async XLA Ops:
  7.2 2.4 copy-start
  11.6 3.6 copy-start.7
  22.3 37.3 %copy-start.10 = (s32[64,8]{0,1:T(8,128)S(1)}, s32[64,8]{0,1:T(8,128)}, u32[]{:S(2)}) copy-start(s32[64,8]{0,1:T(8,128)} %param.10) | copy-start | bytes 6148
  22.3 37.5 %copy-start.9 = (bf16[64,896]{1,0:T(8,128)(2,1)S(1)}, bf16[64,896]{1,0:T(8,128)(2,1)}, u32[]{:S(2)}) copy-start(bf16[64,896]{1,0:T(8,128)(2,1)} %param.9) | copy-start | bytes 344068
  52.3 37.5 %all-to-all-start.1 = ((bf16[32,224,128]{2,1,0:T(8,128)(2,1)}), bf16[32,224,128]{2,1,0:T(8,128)(2,1)S(1)}, u32[]{:S(2)}, u32[]{:S(2)}) async-start(bf16[32,224,128]{2,1,0:T(8,128)(2,1)} %get-tuple-element.74), calls=%async_computation.1 | async-start | bytes 3670016 | tf_op jit(solution)/shard_map/all_to_all | solution.py:35
  59.6 39.7 %copy-start.8 = (s32[32]{0:T(128)S(1)}, s32[32]{0:T(128)}, u32[]{:S(2)}) copy-start(s32[32]{0:T(128)} %param.12) | copy-start | bytes 388
  89.8 9.4 %copy-start.5 = (bf16[32,224,128]{2,1,0:T(8,128)(2,1)}, bf16[32,224,128]{2,1,0:T(8,128)(2,1)S(1)}, u32[]{:S(2)}) copy-start(bf16[32,224,128]{2,1,0:T(8,128)(2,1)S(1)} %all-to-all-done.1) | copy-start | bytes 5505028
  89.8 43.1 %all-to-all-start = ((bf16[32,224,128]{2,1,0:T(8,128)(2,1)}), bf16[32,224,128]{2,1,0:T(8,128)(2,1)}, u32[]{:S(2)}, u32[]{:S(2)}) async-start(bf16[32,224,128]{2,1,0:T(8,128)(2,1)} %get-tuple-element.75), calls=%async_computation | async-start | bytes 3670016 | tf_op jit(solution)/shard_map/all_to_all | solution.py:34
  133.0 137.8 %all-to-all-start.3 = ((bf16[32,24,7168]{2,1,0:T(8,128)(2,1)}), bf16[32,24,7168]{2,1,0:T(8,128)(2,1)}, u32[]{:S(2)}, u32[]{:S(2)}) async-start(bf16[32,24,7168]{2,1,0:T(8,128)(2,1)} %bitcast.188), calls=%async_computation.3 | async-start | bytes 22020096 | tf_op jit(solution)/shard_map/all_to_all | solution.py:59
  140.4 5.1 copy-start.4
  140.4 496.3 %reduce-scatter.4.cloned.1.call-start = ((), (), s32[]{:S(2)}) async-start(), calls=%async_computation.6 | async-start | bytes 12386304
  343.4 29.4 %copy-start.6 = (bf16[32,224,128]{2,1,0:T(8,128)(2,1)S(1)}, bf16[32,224,128]{2,1,0:T(8,128)(2,1)}, u32[]{:S(2)}) copy-start(bf16[32,224,128]{2,1,0:T(8,128)(2,1)} %divide_convert_fusion.2) | copy-start | bytes 5505028
  512.6 0.7 copy-start.11
  513.5 3.7 copy-start.3
  516.4 4.9 copy-start.2
  659.8 25.1 %all-to-all-start.4 = ((bf16[32,1,24,896]{3,2,1,0:T(8,128)(2,1)}), bf16[32,1,24,896]{3,2,1,0:T(8,128)(2,1)S(1)}, u32[]{:S(2)}, u32[]{:S(2)}) async-start(bf16[32,1,24,896]{3,2,1,0:T(8,128)(2,1)} %bitcast.193), calls=%async_computation.4 | async-start | bytes 2752512 | tf_op jit(solution)/shard_map/all_to_all | solution.py:93
  667.2 19.1 %copy-start.1 = (bf16[32,224,128]{2,1,0:T(8,128)(2,1)S(1)}, bf16[32,224,128]{2,1,0:T(8,128)(2,1)}, u32[]{:S(2)}) copy-start(bf16[32,224,128]{2,1,0:T(8,128)(2,1)} %param.15) | copy-start | bytes 5505028
Sparse Core Ops, SparseCore 0:
  512.7 123.9 reduce-scatter.3
where the time goes:
time: 707 us; the launch traced here: 693 us
  waiting for transfers between devices  238 us (34%)
  local copies, waits for them, and re-layouts  191 us (27%)
  matrix products  98.7 us (14%)
  other arithmetic  61.1 us (9%)
  blocking collectives  60.1 us (9%)
  starting transfers between devices  29.9 us (4%)
  between operations  14.5 us (2%)
    unnamed x31, local copies, waits for them, and re-layouts  168 us
    all_to_all x1, waiting for transfers between devices, local(): lax.all_to_all(outgoing, 'dp', split_axis=0, concat_axis=0, tiled=True)  115 us
    unnamed x2, waiting for transfers between devices  112 us
    dot_general x2, matrix products, project(): jnp.einsum('seckgf,ekg->secgf', per_block, scale, precision=lax.Precision...  58.4 us
    dot_general x2, matrix products, project(): jnp.einsum('seckb,ekbgf->seckgf', arrived, quant.reshape(per_owner, D //...  33.2 us
    all_to_all x1, blocking collectives, local(): lax.all_to_all(ordered[2], 'dp', split_axis=0, concat_axis=1, tiled=True)  30.1 us
    all_gather x1, blocking collectives, local(): whole = lax.all_gather(tokens, 'mp', axis=1, tiled=True)  30 us
    gather x3, other arithmetic, local(): target = jnp.take(placement_of, flat) * CAP + position  20.2 us
  transfers between devices with their start and end apart: 5, of which 3 were waited for; matrix products, arithmetic and copies ran while one was open for 10% of the time, Pallas kernels for 0%

commit v1 on v0

v1 whole, which is shorter than its diff:
```python
import jax
import jax.numpy as jnp
from jax import lax
from jax.experimental import pallas as pl
from jax.experimental.pallas import tpu as pltpu
from jax.sharding import PartitionSpec as P

BLK = 128
CAP = 24
EPS = 1e-06
NY, NX = 4, 4
NCH = 4
EARLY = 16
MESH = pl.DeviceIdType.MESH
F32, BF16 = jnp.float32, jnp.bfloat16


def routed_kernel(
    inv, ids4, rw4, tok, wg, wu, wd,
    fresh, mix,
    wog, wou, wod, wsg, wsu, wsd, packed, ids_all, pos_all, slot_w, tz, xs, xg, part,
    rg, ru, qg, qu, r2g, r2u, hid, outp, ob, zb,
    loc, ids_s, ids_r, z_s, z_r, t_s, t_r, w_s, w_r, r1_s, r1_r, r2_s, r2_r, a1_s, a2_s, a_r,
    o_s, o_r, zo_s, zo_r, f_s, f_r,
):
    dp, j = lax.axis_index("dp"), lax.axis_index("mp")
    n_dp, n_z = lax.axis_size("dp"), lax.axis_size("mp")
    nc = NX * NY
    c, h = dp // 2, dp % 2
    y, x = c // NX, c % NX
    sib = 2 * c + 1 - h
    n_e, dr, _ = wog.shape
    per = tz.shape[0] // n_z
    lanes = ids4.shape[1]
    tg = lanes // NX
    eb = n_e // NCH
    rows_ch = eb * CAP
    slots = n_e * CAP
    dc = 2 * dr

    def at(chip):
        return {"dp": 2 * chip + h, "mp": j}

    def remote(src, dst, ss, rs, dev):
        return pltpu.make_async_remote_copy(src_ref=src, dst_ref=dst, send_sem=ss, recv_sem=rs, device_id=dev, device_id_type=MESH)

    own_w = [pltpu.make_async_copy(a, b, loc.at[i]) for i, (a, b) in enumerate(((wg, wog), (wu, wou), (wd, wod)))]
    for cp in own_w:
        cp.start()
    own_tok = pltpu.make_async_copy(tok, tz.at[pl.ds(per * j, per)], loc.at[3])
    own_tok.start()

    lane_g = sum([(lax.broadcasted_iota(jnp.int32, (1, lanes), 1) >= i * tg).astype(jnp.int32) for i in range(1, NX)], jnp.zeros((1, lanes), jnp.int32))
    mine = jnp.where(lane_g == x, ids4[...], -1)
    ids_all[c] = mine

    barrier = pltpu.get_barrier_semaphore()

    def greet(k, _):
        pl.semaphore_signal(barrier, inc=1, device_id={"dp": (dp + k) % n_dp, "mp": j}, device_id_type=MESH)
        return 0

    lax.fori_loop(1, n_dp, greet, 0)

    def greet_z(k, _):
        pl.semaphore_signal(barrier, inc=1, device_id={"dp": dp, "mp": (j + k) % n_z}, device_id_type=MESH)
        return 0

    lax.fori_loop(1, n_z, greet_z, 0)
    pl.semaphore_wait(barrier, n_dp + n_z - 2)

    def z_copy(k):
        to = (j + k) % n_z
        return remote(tok, tz.at[pl.ds(per * j, per)], z_s.at[k], z_r.at[k], {"dp": dp, "mp": to})

    def z_start(k, _):
        z_copy(k).start()
        return 0

    lax.fori_loop(1, n_z, z_start, 0)

    def ids_copy(k):
        return remote(ids_all.at[c], ids_all.at[c], ids_s.at[k], ids_r.at[k], at((c + k) % nc))

    def ids_start(k, _):
        ids_copy(k).start()
        return 0

    lax.fori_loop(1, nc, ids_start, 0)
    sib_w = [
        remote(a, b, w_s.at[i], w_r.at[i], {"dp": sib, "mp": j})
        for i, (a, b) in enumerate(((wg, wsg), (wu, wsu), (wd, wsd)))
    ]
    for cp in sib_w:
        cp.start()

    for cp in own_w:
        cp.wait()

    def pack(s, _):
        e = inv[s]
        packed[s, 0] = wog[e]
        packed[s, 1] = wou[e]
        packed[s, 2] = wod[e]
        return 0

    lax.fori_loop(0, n_e, pack, 0)
    own_fresh = pltpu.make_async_copy(packed.at[dp], fresh.at[dp], loc.at[0])
    own_fresh.start()

    def f_copy(k):
        to = (dp + k) % n_dp
        return remote(packed.at[to], fresh.at[dp], f_s.at[k], f_r.at[k], {"dp": to, "mp": j})

    def f_start(k, _):
        f_copy(k).start()
        return 0

    early = min(EARLY, n_dp)
    lax.fori_loop(1, early, f_start, 0)

    lane_i = lax.broadcasted_iota(jnp.int32, (lanes, lanes), 1)
    row_i = lax.broadcasted_iota(jnp.int32, (lanes, lanes), 0)
    lane_of = sum([(lane_i >= i * tg).astype(jnp.int32) for i in range(1, NX)], jnp.zeros((lanes, lanes), jnp.int32))
    row_of = sum([(row_i >= i * tg).astype(jnp.int32) for i in range(1, NX)], jnp.zeros((lanes, lanes), jnp.int32))
    before = jnp.where((row_i < lane_i) & (lane_of == row_of), 1.0, 0.0).astype(BF16)
    e_iota = lax.broadcasted_iota(jnp.int32, (n_e, lanes), 0)
    top = ids4.shape[0]

    def positions(ids):
        named = jnp.zeros((n_e, lanes), F32)
        for i in range(top):
            named = jnp.where(ids[i : i + 1, :] == e_iota, 1.0, named)
        count = jnp.dot(named.astype(BF16), before, preferred_element_type=F32)
        return jnp.where(named > 0.5, count, -1.0)

    my_pos = positions(mine)
    my_w = jnp.zeros((n_e, lanes), F32)
    for i in range(top):
        my_w = jnp.where(mine[i : i + 1, :] == e_iota, rw4[i : i + 1, :], my_w)
    p_iota = lax.broadcasted_iota(jnp.int32, (CAP, lanes), 0).astype(F32)
    for q in range(NCH):
        pe = my_pos[q * eb : (q + 1) * eb, :].reshape(eb, 1, lanes)
        we = my_w[q * eb : (q + 1) * eb, :].reshape(eb, 1, lanes)
        ws = jnp.sum(jnp.where(pe == p_iota[None], we, 0.0), axis=2, keepdims=True)
        slot_w[q * rows_ch : (q + 1) * rows_ch, :] = jnp.broadcast_to(ws.reshape(rows_ch, 1), (rows_ch, BLK))

    own_tok.wait()

    def z_wait(k, _):
        src = (j + n_z - k) % n_z
        remote(tok, tz.at[pl.ds(per * src, per)], z_s.at[k], z_r.at[k], {"dp": dp, "mp": src}).wait_recv()
        return 0

    lax.fori_loop(1, n_z, z_wait, 0)

    def t_copy(k):
        to = (c + k) % nc
        return remote(tz.at[to], xs.at[c], t_s.at[k], t_r.at[k], at(to))

    def t_start(k, _):
        t_copy(k).start()
        return 0

    lax.fori_loop(1, nc, t_start, 0)
    own_x = pltpu.make_async_copy(tz.at[c], xs.at[c], loc.at[3])
    own_x.start()

    def ids_wait(k, _):
        src = (c + nc - k) % nc
        remote(ids_all.at[src], ids_all.at[src], ids_s.at[k], ids_r.at[k], at(src)).wait_recv()
        return 0

    lax.fori_loop(1, nc, ids_wait, 0)

    def place(b, _):
        ids = ids_all[b * NX]
        for i in range(1, NX):
            ids = jnp.maximum(ids, ids_all[b * NX + i])
        pos_all[b] = positions(ids)
        return 0

    lax.fori_loop(0, NY, place, 0)
    own_x.wait()

    def t_wait(k, _):
        src = (c + nc - k) % nc
        remote(tz.at[src], xs.at[src], t_s.at[k], t_r.at[k], at(src)).wait_recv()
        return 0

    lax.fori_loop(1, nc, t_wait, 0)
    for cp in sib_w:
        cp.wait_recv()

    r_iota = lax.broadcasted_iota(jnp.int32, (NX * CAP, lanes), 0)
    r_of = sum([(r_iota >= i * CAP).astype(jnp.int32) for i in range(1, NX)], jnp.zeros((NX * CAP, lanes), jnp.int32))
    want = jnp.where(r_of == lane_g, r_iota - CAP * r_of, -9).astype(F32)

    def one_hot(b, q):
        pe = pos_all[b, pl.ds(pl.multiple_of(q * eb, eb), eb), :].reshape(eb, 1, lanes)
        hot = jnp.where(pe == want[None], 1.0, 0.0).astype(BF16)
        return hot.reshape(eb * NX * CAP, lanes)

    def pick(q, b):
        tokens = xs[pl.ds(b * NX, NX)].reshape(lanes, dc)
        got = jnp.dot(one_hot(b, q), tokens, preferred_element_type=F32)
        xg[pl.ds(q * eb, eb), b] = got.astype(BF16).reshape(eb, NX * CAP, dc)

    def project(e):
        a = xg[e].reshape(NY * NX * CAP, dc)
        w = jnp.concatenate(
            [
                jnp.concatenate([wog[e], wou[e]], axis=1),
                jnp.concatenate([wsg[e], wsu[e]], axis=1),
            ],
            axis=0,
        )
        return jnp.dot(a, w, preferred_element_type=F32).reshape(nc, CAP, 2 * BLK)

    def rows_of(q):
        return pl.ds(pl.multiple_of(q * rows_ch, rows_ch), rows_ch)

    def r1_copy(q, k, up):
        if up:
            to = (y + k) % NY
            return remote(part.at[to, :, rows_of(q), pl.ds(BLK, BLK)], ru.at[k - 1, :, rows_of(q), :], r1_s.at[1, q, k - 1], r1_r.at[1, q, k - 1], at(to * NX + x))
        to = (x + k) % NX
        return remote(part.at[:, to, rows_of(q), pl.ds(0, BLK)], rg.at[k - 1, :, rows_of(q), :], r1_s.at[0, q, k - 1], r1_r.at[0, q, k - 1], at(y * NX + to))

    def first(q, _):
        for b in range(NY):
            pick(q, b)

        def pair(i, _):
            e = q * eb + 2 * i
            both = jnp.concatenate([project(e), project(e + 1)], axis=1).astype(BF16)
            part[:, :, pl.ds(pl.multiple_of(e * CAP, 2 * CAP), 2 * CAP), :] = both.reshape(NY, NX, 2 * CAP, 2 * BLK)
            return 0

        lax.fori_loop(0, eb // 2, pair, 0)
        for k in range(1, NX):
            r1_copy(q, k, False).start()
        for k in range(1, NY):
            r1_copy(q, k, True).start()
        return 0

    lax.fori_loop(0, NCH, first, 0)

    def r2_copy(q, k, up):
        if up:
            to = (x + k) % NX
            return remote(qu.at[to, rows_of(q), :], r2u.at[k - 1, rows_of(q), :], r2_s.at[1, q, k - 1], r2_r.at[1, q, k - 1], at(y * NX + to))
        to = (y + k) % NY
        return remote(qg.at[to, rows_of(q), :], r2g.at[k - 1, rows_of(q), :], r2_s.at[0, q, k - 1], r2_r.at[0, q, k - 1], at(to * NX + x))

    def second(q, _):
        rows = rows_of(q)
        for k in range(1, NX):
            r1_copy(q, k, False).wait_recv()

        def sum_g(i, _):
            t = part[i, x, rows, pl.ds(0, BLK)].astype(F32)
            for k in range(NX - 1):
                t = t + rg[k, i, rows, :].astype(F32)
            qg[i, rows, :] = t.astype(BF16)
            return 0

        lax.fori_loop(0, NY, sum_g, 0)
        for k in range(1, NY):
            r2_copy(q, k, False).start()
        for k in range(1, NY):
            r1_copy(q, k, True).wait_recv()

        def sum_u(i, _):
            t = part[y, i, rows, pl.ds(BLK, BLK)].astype(F32)
            for k in range(NY - 1):
                t = t + ru[k, i, rows, :].astype(F32)
            qu[i, rows, :] = t.astype(BF16)
            return 0

        lax.fori_loop(0, NX, sum_u, 0)
        for k in range(1, NX):
            r2_copy(q, k, True).start()
        return 0

    lax.fori_loop(0, NCH, second, 0)

    def line(q_along_x, k):
        if q_along_x:
            return y * NX + (x + k) % NX
        return ((y + k) % NY) * NX + x

    def a_copy(q, src, dev, ss):
        sl = hid.at[src // NX, src % NX, rows_of(q), :]
        return remote(sl, sl, ss, a_r.at[q, src], dev)

    def third(along_x):
        n1, n2 = (NX, NY) if along_x else (NY, NX)

        def body(q, _):
            rows = rows_of(q)
            for k in range(1, NY):
                r2_copy(q, k, False).wait_recv()
            for k in range(1, NX):
                r2_copy(q, k, True).wait_recv()
            gate = qg[y, rows, :].astype(F32)
            for k in range(NY - 1):
                gate = gate + r2g[k, rows, :].astype(F32)
            up = qu[x, rows, :].astype(F32)
            for k in range(NX - 1):
                up = up + r2u[k, rows, :].astype(F32)
            value = gate / (1.0 + jnp.exp(-gate)) * up * slot_w[rows, :]
            hid[y, x, rows, :] = value.astype(BF16)
            for k in range(1, n1):
                a_copy(q, c, at(line(along_x, k)), a1_s.at[q, k]).start()
            for k in range(1, n2):
                a_copy(q, c, at(line(not along_x, k)), a2_s.at[q, 0, k]).start()
            return 0

        return body

    half = NCH // 2
    lax.fori_loop(0, half, third(True), 0)
    lax.fori_loop(half, NCH, third(False), 0)

    def forward(along_x):
        n1, n2 = (NX, NY) if along_x else (NY, NX)

        def body(q, _):
            for k in range(1, n1):
                src = line(along_x, n1 - k)
                a_copy(q, src, at(src), a1_s.at[q, k]).wait_recv()
                for m in range(1, n2):
                    a_copy(q, src, at(line(not along_x, m)), a2_s.at[q, k, m]).start()
            return 0

        return body

    lax.fori_loop(0, half, forward(True), 0)
    lax.fori_loop(half, NCH, forward(False), 0)
    lax.fori_loop(early, n_dp, f_start, 0)

    def down(along_x):
        n1, n2 = (NX, NY) if along_x else (NY, NX)

        def body(q, _):
            for m in range(1, n2):
                for k in range(n1):
                    if along_x:
                        src = ((y + m) % NY) * NX + (x + k) % NX
                    else:
                        src = ((y + k) % NY) * NX + (x + m) % NX
                    a_copy(q, src, at(src), a1_s.at[q, 0]).wait_recv()

            def pair(i, _):
                e = q * eb + 2 * i
                both = hid[:, :, pl.ds(pl.multiple_of(e * CAP, 2 * CAP), 2 * CAP), :].astype(F32).reshape(nc, 2 * CAP, BLK)
                for o in range(2):
                    a = both[:, o * CAP : (o + 1) * CAP, :].reshape(nc * CAP, BLK).astype(BF16)
                    w = jnp.concatenate([wod[e + o], wsd[e + o]], axis=0)
                    got = lax.dot_general(a, w, (((1,), (1,)), ((), ())), preferred_element_type=F32)
                    xg[e + o] = got.astype(BF16).reshape(NY, NX * CAP, dc)
                return 0

            lax.fori_loop(0, eb // 2, pair, 0)
            return 0

        return body

    lax.fori_loop(0, half, down(True), 0)
    lax.fori_loop(half, NCH, down(False), 0)

    def o_copy(to):
        k = (to + nc - c) % nc
        return remote(outp.at[to], ob.at[c], o_s.at[k], o_r.at[k], at(to))

    def combine(b, _):
        total = jnp.zeros((lanes, dc), F32)
        for q in range(NCH):
            d = xg[pl.ds(q * eb, eb), b].reshape(eb * NX * CAP, dc)
            total = total + lax.dot_general(one_hot(b, q), d, (((0,), (0,)), ((), ())), preferred_element_type=F32)
        outp[pl.ds(b * NX, NX)] = total.astype(BF16).reshape(NX, tg, dc)
        for i in range(NX):
            to = b * NX + i

            @pl.when(to != c)
            def _():
                o_copy(to).start()

        return 0

    lax.fori_loop(0, NY, combine, 0)
    ob[c] = outp[c]

    def o_wait(k, _):
        src = (c + nc - k) % nc
        remote(outp.at[src], ob.at[src], o_s.at[k], o_r.at[k], at(src)).wait_recv()
        return 0

    lax.fori_loop(1, nc, o_wait, 0)

    def zo_copy(k):
        to = (j + k) % n_z
        return remote(ob.at[pl.ds(per * to, per)], zb.at[k], zo_s.at[k], zo_r.at[k], {"dp": dp, "mp": to})

    def zo_start(k, _):
        zo_copy(k).start()
        return 0

    lax.fori_loop(1, n_z, zo_start, 0)
    total = ob[pl.ds(per * j, per)].astype(F32)
    for k in range(1, n_z):
        zo_copy(k).wait_recv()
        total = total + zb[k].astype(F32)
    mix[...] = total.astype(BF16)

    own_fresh.wait()

    def f_wait(k, _):
        src = (dp + n_dp - k) % n_dp
        remote(packed.at[src], fresh.at[src], f_s.at[k], f_r.at[k], {"dp": src, "mp": j}).wait_recv()
        f_copy(k).wait_send()
        return 0

    lax.fori_loop(1, n_dp, f_wait, 0)

    def z_done(k, _):
        z_copy(k).wait_send()
        zo_copy(k).wait_send()
        return 0

    lax.fori_loop(1, n_z, z_done, 0)

    def plane_done(k, _):
        ids_copy(k).wait_send()
        t_copy(k).wait_send()
        o_copy((c + k) % nc).wait_send()
        return 0

    lax.fori_loop(1, nc, plane_done, 0)
    for cp in sib_w:
        cp.wait_send()

    def sums_done(q, _):
        for k in range(1, NX):
            r1_copy(q, k, False).wait_send()
            r2_copy(q, k, True).wait_send()
        for k in range(1, NY):
            r1_copy(q, k, True).wait_send()
            r2_copy(q, k, False).wait_send()
        return 0

    lax.fori_loop(0, NCH, sums_done, 0)

    def hid_done(along_x):
        n1, n2 = (NX, NY) if along_x else (NY, NX)

        def body(q, _):
            for k in range(1, n1):
                a_copy(q, c, at(c), a1_s.at[q, k]).wait_send()
            for k in range(n1):
                for m in range(1, n2):
                    a_copy(q, c, at(c), a2_s.at[q, k, m]).wait_send()
            return 0

        return body

    lax.fori_loop(0, half, hid_done(True), 0)
    lax.fori_loop(half, NCH, hid_done(False), 0)


def quantize_kernel(fresh, gate, up, down, scales):
    rows = gate.shape[1]
    for m, out in enumerate((gate, up, down)):
        w = fresh[:, m].reshape(rows // BLK, BLK, BLK).astype(F32)
        top = jnp.max(jnp.max(jnp.abs(w), axis=1, keepdims=True), axis=2, keepdims=True) + EPS
        out[0] = (w / top).astype(BF16).reshape(rows, BLK)
        scales[0, m] = jnp.broadcast_to(top, (rows // BLK, 1, BLK)).reshape(rows // BLK, BLK)


def local(tokens, expert_ids, route_weights, placement_of, gate_weight, up_weight, down_weight):
    n_dp, n_z = lax.axis_size("dp"), lax.axis_size("mp")
    nc = n_dp // 2
    n_e, dr, _ = gate_weight.shape
    tg, wide = tokens.shape
    top = expert_ids.shape[1]
    dc, per, lanes = 2 * dr, wide // (2 * dr), NX * tg
    slots = n_e * CAP
    h = lax.axis_index("dp") % 2

    order = jnp.arange(n_e, dtype=jnp.int32)
    inv = jnp.sum(jnp.where(placement_of[:, None] == order[None, :], order[:, None], 0), axis=0)
    pieces = tokens.reshape(tg, per, 2, dr)
    pieces = jnp.where(h == 0, pieces, pieces[:, :, ::-1]).reshape(tg, per, dc).transpose(1, 0, 2)
    ids4 = jnp.tile(expert_ids.T, (1, NX))
    rw4 = jnp.tile(route_weights.T, (1, NX))

    vm = pltpu.VMEM
    dma = pltpu.SemaphoreType.DMA
    hbm = pl.BlockSpec(memory_space=pl.ANY)
    vmem = pl.BlockSpec(memory_space=pltpu.VMEM)
    weights = [vm((n_e, dr, BLK), BF16)] * 6
    fresh, mix = pl.pallas_call(
        routed_kernel,
        out_shape=(
            jax.ShapeDtypeStruct((n_dp, 3, dr, BLK), BF16),
            jax.ShapeDtypeStruct((per, tg, dc), BF16),
        ),
        in_specs=[pl.BlockSpec(memory_space=pltpu.SMEM), vmem, vmem, vmem, hbm, hbm, hbm],
        out_specs=(hbm, vmem),
        scratch_shapes=weights
        + [
            vm((n_dp, 3, dr, BLK), BF16),
            vm((nc, top, lanes), jnp.int32),
            vm((NY, n_e, lanes), F32),
            vm((slots, BLK), F32),
            vm((nc, tg, dc), BF16),
            vm((nc, tg, dc), BF16),
            vm((n_e, NY, NX * CAP, dc), BF16),
            vm((NY, NX, slots, 2 * BLK), BF16),
            vm((NX - 1, NY, slots, BLK), BF16),
            vm((NY - 1, NX, slots, BLK), BF16),
            vm((NY, slots, BLK), BF16),
            vm((NX, slots, BLK), BF16),
            vm((NY - 1, slots, BLK), BF16),
            vm((NX - 1, slots, BLK), BF16),
            vm((NY, NX, slots, BLK), BF16),
            vm((nc, tg, dc), BF16),
            vm((nc, tg, dc), BF16),
            vm((n_z, per, tg, dc), BF16),
            dma((4,)),
            dma((nc,)), dma((nc,)),
            dma((n_z,)), dma((n_z,)),
            dma((nc,)), dma((nc,)),
            dma((3,)), dma((3,)),
            dma((2, NCH, 3)), dma((2, NCH, 3)),
            dma((2, NCH, 3)), dma((2, NCH, 3)),
            dma((NCH, 4)), dma((NCH, 4, 4)), dma((NCH, nc)),
            dma((nc,)), dma((nc,)),
            dma((n_z,)), dma((n_z,)),
            dma((n_dp,)), dma((n_dp,)),
        ],
        compiler_params=pltpu.CompilerParams(collective_id=0, has_side_effects=True, vmem_limit_bytes=62 * 1024 * 1024),
    )(inv, ids4, rw4, pieces, gate_weight, up_weight, down_weight)

    step = max(1, BLK // dr if dr < BLK else 4)
    rows = step * dr
    grid = n_dp // step
    out_w = jax.ShapeDtypeStruct((1, n_dp * dr, BLK), BF16)
    spec_w = pl.BlockSpec((1, rows, BLK), lambda i: (0, i, 0))
    gate_q, up_q, down_q, scales = pl.pallas_call(
        quantize_kernel,
        grid=(grid,),
        out_shape=(out_w, out_w, out_w, jax.ShapeDtypeStruct((grid, 3, rows // BLK, BLK), F32)),
        in_specs=[pl.BlockSpec((step, 3, dr, BLK), lambda i: (i, 0, 0, 0))],
        out_specs=(spec_w, spec_w, spec_w, pl.BlockSpec((1, 3, rows // BLK, BLK), lambda i: (i, 0, 0, 0))),
    )(fresh)
    scales = scales[:, :, :, 0].transpose(1, 0, 2).reshape(3, 1, -1, 1)

    mixed = mix.transpose(1, 0, 2).reshape(tg, per, 2, dr)
    mixed = jnp.where(h == 0, mixed, mixed[:, :, ::-1]).reshape(tg, wide)
    return gate_q, up_q, down_q, scales, mixed


def solution(mesh):
    placed = (
        P("dp", "mp"),
        P("dp", None),
        P("dp", None),
        P(),
        P(None, "dp", "mp"),
        P(None, "dp", "mp"),
        P(None, "dp", "mp"),
    )
    return jax.shard_map(
        local,
        mesh=mesh,
        in_specs=placed,
        out_specs=(
            P("dp", None, "mp"),
            P("dp", None, "mp"),
            P("dp", None, "mp"),
            P(None, "dp", None, "mp"),
            P("dp", "mp"),
        ),
        check_vma=False,
    )
```

time: 707 us -> 262 us (0.37)
  the two profiles are of different devices: /device:TPU:10 before, /device:TPU:24 now
where the time goes in v1:
time: 262 us
  Pallas kernels  250 us (95%)
  local copies, waits for them, and re-layouts  9.82 us (4%)
    pallas_call x1, Pallas kernels, local(): pl.pallas_call(routed_kernel, out_shape=(jax.ShapeDtypeStruct((n_dp, 3, d...  242 us
    pallas_call x1, Pallas kernels, local(): pl.pallas_call(quantize_kernel, grid=(grid,), out_shape=(out_w, out_w, ou...  7.84 us

profile of v1, /device:TPU:24, one launch (start us, length us, event | category | flops | bytes accessed | tf_op | source)
XLA Modules:
  0.0 261.6 jit_solution(6991317394966261468)
XLA Ops:
  0.6 1.1 reshape.34
  1.7 0.1 copy.21
  1.8 0.7 rev.6
  2.5 0.1 broadcast_select_fusion.1
  2.7 0.8 reshape.35
  3.5 0.7 tile.20
  4.2 0.7 tile.21.rw4
  4.8 0.7 tile.8
  5.5 0.7 tile.9.ids4
  6.2 1.3 select_reduce_fusion.inv
  7.5 241.8 %shard_map.110 = (bf16[32,3,224,128]{3,2,1,0:T(8,128)(2,1)}, bf16[2,64,448]{2,1,0:T(8,128)(2,1)}) custom-call(s32[32]{0:T(128)} %select_reduce_fusion.inv, s32[8,256]{1,0:T(8,128)} %tile.9.ids4, f32[8,256]{1,0:T(8,128)} %tile.21.rw4, bf16[2,64,448]{2,1,0:T(8,128)(2,1)} %bitcast.16, bf16[32,224,128]{2,1,0:T(8,128)(2,1)} %wg.1, bf16[32,224,128]{2,1,0:T(8,128)(2,1)} %wu.1, ...), custom_call_target="tpu_custom_call" | custom-call | tf_op jit(solution)/shard_map/pallas_call | solution.py:503
  249.3 1.0 reshape.37
  250.3 0.7 rev.7
  251.0 0.1 copy.23
  251.1 0.8 reshape.38
  251.9 7.8 %shard_map.111 = (bf16[1,7168,128]{2,1,0:T(8,128)(2,1)}, bf16[1,7168,128]{2,1,0:T(8,128)(2,1)}, bf16[1,7168,128]{2,1,0:T(8,128)(2,1)}, f32[8,3,7,128]{3,2,1,0:T(8,128)}) custom-call(bf16[32,3,224,128]{3,2,1,0:T(8,128)(2,1)} %get-tuple-element.11.fresh), custom_call_target="tpu_custom_call" | custom-call | tf_op jit(solution)/shard_map/pallas_call | solution.py:551
  259.8 1.1 copy.22
  260.9 0.6 reshape.39
  (1 shorter events, 0.0 us)

commit v2 on v1

--- a/solution.py
+++ b/solution.py
@@ -10,18 +10,18 @@
 EPS = 1e-06
 NY, NX = 4, 4
 NCH = 4
-EARLY = 16
+EARLY = 1
 MESH = pl.DeviceIdType.MESH
 F32, BF16 = jnp.float32, jnp.bfloat16
 
 
 def routed_kernel(
-    inv, ids4, rw4, tok, wg, wu, wd,
+    inv, ids, rw, tok, wg, wu, wd,
     fresh, mix,
-    wog, wou, wod, wsg, wsu, wsd, packed, ids_all, pos_all, slot_w, tz, xs, xg, part,
+    wog, wou, wod, wsg, wsu, wsd, packed, st_a, st_b, tokp, ids_all, pos_all, slot_w, tz, xs, xg, part,
     rg, ru, qg, qu, r2g, r2u, hid, outp, ob, zb,
     loc, ids_s, ids_r, z_s, z_r, t_s, t_r, w_s, w_r, r1_s, r1_r, r2_s, r2_r, a1_s, a2_s, a_r,
-    o_s, o_r, zo_s, zo_r, f_s, f_r,
+    o_s, o_r, zo_s, zo_r, f1_s, f1_r, f2_s, f2_r,
 ):
     dp, j = lax.axis_index("dp"), lax.axis_index("mp")
     n_dp, n_z = lax.axis_size("dp"), lax.axis_size("mp")
@@ -31,8 +31,8 @@
     sib = 2 * c + 1 - h
     n_e, dr, _ = wog.shape
     per = tz.shape[0] // n_z
-    lanes = ids4.shape[1]
-    tg = lanes // NX
+    top, tg = ids.shape
+    lanes = NX * tg
     eb = n_e // NCH
     rows_ch = eb * CAP
     slots = n_e * CAP
@@ -47,11 +47,13 @@
     own_w = [pltpu.make_async_copy(a, b, loc.at[i]) for i, (a, b) in enumerate(((wg, wog), (wu, wou), (wd, wod)))]
     for cp in own_w:
         cp.start()
-    own_tok = pltpu.make_async_copy(tok, tz.at[pl.ds(per * j, per)], loc.at[3])
+    for i in range(per):
+        tokp[i] = tok[:, i * dc : (i + 1) * dc]
+    own_tok = pltpu.make_async_copy(tokp, tz.at[pl.ds(per * j, per)], loc.at[3])
     own_tok.start()
 
     lane_g = sum([(lax.broadcasted_iota(jnp.int32, (1, lanes), 1) >= i * tg).astype(jnp.int32) for i in range(1, NX)], jnp.zeros((1, lanes), jnp.int32))
-    mine = jnp.where(lane_g == x, ids4[...], -1)
+    mine = jnp.where(lane_g == x, jnp.concatenate([ids[...]] * NX, axis=1), -1)
     ids_all[c] = mine
 
     barrier = pltpu.get_barrier_semaphore()
@@ -71,7 +73,7 @@
 
     def z_copy(k):
         to = (j + k) % n_z
-        return remote(tok, tz.at[pl.ds(per * j, per)], z_s.at[k], z_r.at[k], {"dp": dp, "mp": to})
+        return remote(tokp, tz.at[pl.ds(per * j, per)], z_s.at[k], z_r.at[k], {"dp": dp, "mp": to})
 
     def z_start(k, _):
         z_copy(k).start()
@@ -99,25 +101,71 @@
 
     def pack(s, _):
         e = inv[s]
-        packed[s, 0] = wog[e]
-        packed[s, 1] = wou[e]
-        packed[s, 2] = wod[e]
+        to = (s // (2 * NX), (s // 2) % NX, s % 2)
+        packed[to[0], to[1], to[2], 0] = wog[e]
+        packed[to[0], to[1], to[2], 1] = wou[e]
+        packed[to[0], to[1], to[2], 2] = wod[e]
         return 0
 
     lax.fori_loop(0, n_e, pack, 0)
-    own_fresh = pltpu.make_async_copy(packed.at[dp], fresh.at[dp], loc.at[0])
-    own_fresh.start()
-
-    def f_copy(k):
-        to = (dp + k) % n_dp
-        return remote(packed.at[to], fresh.at[dp], f_s.at[k], f_r.at[k], {"dp": to, "mp": j})
-
-    def f_start(k, _):
-        f_copy(k).start()
-        return 0
-
-    early = min(EARLY, n_dp)
-    lax.fori_loop(1, early, f_start, 0)
+    hr = dr // 2
+    top_rows, low_rows = pl.ds(0, hr), pl.ds(hr, hr)
+
+    def f1_copy(k, low):
+        if low:
+            to = (y + k) % NY
+            return remote(packed.at[to, :, :, :, low_rows, :], st_b.at[y], f1_s.at[1, k - 1], f1_r.at[1, k - 1], at(to * NX + x))
+        to = (x + k) % NX
+        return remote(packed.at[:, to, :, :, top_rows, :], st_a.at[x], f1_s.at[0, k - 1], f1_r.at[0, k - 1], at(y * NX + to))
+
+    def f1_from(k, low):
+        if low:
+            src = (y + NY - k) % NY
+            return remote(packed.at[y, :, :, :, low_rows, :], st_b.at[src], f1_s.at[1, k - 1], f1_r.at[1, k - 1], at(src * NX + x))
+        src = (x + NX - k) % NX
+        return remote(packed.at[:, x, :, :, top_rows, :], st_a.at[src], f1_s.at[0, k - 1], f1_r.at[0, k - 1], at(y * NX + src))
+
+    f1_own = [
+        pltpu.make_async_copy(packed.at[:, x, :, :, top_rows, :], st_a.at[x], loc.at[4]),
+        pltpu.make_async_copy(packed.at[y, :, :, :, low_rows, :], st_b.at[y], loc.at[5]),
+    ]
+
+    def f2_copy(k, d, low):
+        core = (h + d) % 2
+        if low:
+            to = (x + k) % NX
+            return remote(st_b.at[:, to, core], fresh.at[:, x, h, :, low_rows, :], f2_s.at[1, k, d], f2_r.at[1, k, d], {"dp": 2 * (y * NX + to) + core, "mp": j})
+        to = (y + k) % NY
+        return remote(st_a.at[:, to, core], fresh.at[y, :, h, :, top_rows, :], f2_s.at[0, k, d], f2_r.at[0, k, d], {"dp": 2 * (to * NX + x) + core, "mp": j})
+
+    def f2_from(k, d, low):
+        core = (h + d) % 2
+        if low:
+            src = (x + NX - k) % NX
+            return remote(st_b.at[:, x, h], fresh.at[:, src, core, :, low_rows, :], f2_s.at[1, k, d], f2_r.at[1, k, d], {"dp": 2 * (y * NX + src) + core, "mp": j})
+        src = (y + NY - k) % NY
+        return remote(st_a.at[:, y, h], fresh.at[src, :, core, :, top_rows, :], f2_s.at[0, k, d], f2_r.at[0, k, d], {"dp": 2 * (src * NX + x) + core, "mp": j})
+
+    f2_own = [
+        pltpu.make_async_copy(st_a.at[:, y, h], fresh.at[y, :, h, :, top_rows, :], loc.at[4]),
+        pltpu.make_async_copy(st_b.at[:, x, h], fresh.at[:, x, h, :, low_rows, :], loc.at[5]),
+    ]
+    steps = [(k, d) for k in range(max(NX, NY)) for d in range(2) if k or d]
+
+    def f2_start(ks):
+        for k, d in steps:
+            if k in ks:
+                if k < NY:
+                    f2_copy(k, d, False).start()
+                if k < NX:
+                    f2_copy(k, d, True).start()
+
+    for cp in f1_own:
+        cp.start()
+    for k in range(1, NX):
+        f1_copy(k, False).start()
+    for k in range(1, NY):
+        f1_copy(k, True).start()
 
     lane_i = lax.broadcasted_iota(jnp.int32, (lanes, lanes), 1)
     row_i = lax.broadcasted_iota(jnp.int32, (lanes, lanes), 0)
@@ -125,7 +173,7 @@
     row_of = sum([(row_i >= i * tg).astype(jnp.int32) for i in range(1, NX)], jnp.zeros((lanes, lanes), jnp.int32))
     before = jnp.where((row_i < lane_i) & (lane_of == row_of), 1.0, 0.0).astype(BF16)
     e_iota = lax.broadcasted_iota(jnp.int32, (n_e, lanes), 0)
-    top = ids4.shape[0]
+    rw4 = jnp.concatenate([rw[...]] * NX, axis=1)
 
     def positions(ids):
         named = jnp.zeros((n_e, lanes), F32)
@@ -149,7 +197,7 @@
 
     def z_wait(k, _):
         src = (j + n_z - k) % n_z
-        remote(tok, tz.at[pl.ds(per * src, per)], z_s.at[k], z_r.at[k], {"dp": dp, "mp": src}).wait_recv()
+        remote(tokp, tz.at[pl.ds(per * src, per)], z_s.at[k], z_r.at[k], {"dp": dp, "mp": src}).wait_recv()
         return 0
 
     lax.fori_loop(1, n_z, z_wait, 0)
@@ -192,6 +240,16 @@
     for cp in sib_w:
         cp.wait_recv()
 
+    for cp in f1_own:
+        cp.wait()
+    for k in range(1, NX):
+        f1_from(k, False).wait_recv()
+    for k in range(1, NY):
+        f1_from(k, True).wait_recv()
+    for cp in f2_own:
+        cp.start()
+    f2_start(range(EARLY))
+
     r_iota = lax.broadcasted_iota(jnp.int32, (NX * CAP, lanes), 0)
     r_of = sum([(r_iota >= i * CAP).astype(jnp.int32) for i in range(1, NX)], jnp.zeros((NX * CAP, lanes), jnp.int32))
     want = jnp.where(r_of == lane_g, r_iota - CAP * r_of, -9).astype(F32)
@@ -206,15 +264,12 @@
         got = jnp.dot(one_hot(b, q), tokens, preferred_element_type=F32)
         xg[pl.ds(q * eb, eb), b] = got.astype(BF16).reshape(eb, NX * CAP, dc)
 
+    def by_core(own, other):
+        return jnp.concatenate([jnp.where(h == 0, own, other), jnp.where(h == 0, other, own)], axis=0)
+
     def project(e):
         a = xg[e].reshape(NY * NX * CAP, dc)
-        w = jnp.concatenate(
-            [
-                jnp.concatenate([wog[e], wou[e]], axis=1),
-                jnp.concatenate([wsg[e], wsu[e]], axis=1),
-            ],
-            axis=0,
-        )
+        w = jnp.concatenate([by_core(wog[e], wsg[e]), by_core(wou[e], wsu[e])], axis=1)
         return jnp.dot(a, w, preferred_element_type=F32).reshape(nc, CAP, 2 * BLK)
 
     def rows_of(q):
@@ -338,7 +393,7 @@
 
     lax.fori_loop(0, half, forward(True), 0)
     lax.fori_loop(half, NCH, forward(False), 0)
-    lax.fori_loop(early, n_dp, f_start, 0)
+    f2_start(range(EARLY, max(NX, NY)))
 
     def down(along_x):
         n1, n2 = (NX, NY) if along_x else (NY, NX)
@@ -357,7 +412,7 @@
                 both = hid[:, :, pl.ds(pl.multiple_of(e * CAP, 2 * CAP), 2 * CAP), :].astype(F32).reshape(nc, 2 * CAP, BLK)
                 for o in range(2):
                     a = both[:, o * CAP : (o + 1) * CAP, :].reshape(nc * CAP, BLK).astype(BF16)
-                    w = jnp.concatenate([wod[e + o], wsd[e + o]], axis=0)
+                    w = by_core(wod[e + o], wsd[e + o])
                     got = lax.dot_general(a, w, (((1,), (1,)), ((), ())), preferred_element_type=F32)
                     xg[e + o] = got.astype(BF16).reshape(NY, NX * CAP, dc)
                 return 0
@@ -374,14 +429,23 @@
         k = (to + nc - c) % nc
         return remote(outp.at[to], ob.at[c], o_s.at[k], o_r.at[k], at(to))
 
-    def combine(b, _):
+    def zo_copy(to):
+        k = (to + n_z - j) % n_z
+        return remote(ob.at[pl.ds(per * to, per)], zb.at[k], zo_s.at[k], zo_r.at[k], {"dp": dp, "mp": to})
+
+    def from_z(k):
+        src = (j + n_z - k) % n_z
+        return remote(ob.at[pl.ds(per * src, per)], zb.at[k], zo_s.at[k], zo_r.at[k], {"dp": dp, "mp": src})
+
+    def combine(i, _):
+        b = (y + 1 + i) % NY
         total = jnp.zeros((lanes, dc), F32)
         for q in range(NCH):
             d = xg[pl.ds(q * eb, eb), b].reshape(eb * NX * CAP, dc)
             total = total + lax.dot_general(one_hot(b, q), d, (((0,), (0,)), ((), ())), preferred_element_type=F32)
         outp[pl.ds(b * NX, NX)] = total.astype(BF16).reshape(NX, tg, dc)
-        for i in range(NX):
-            to = b * NX + i
+        for n in range(NX):
+            to = b * NX + n
 
             @pl.when(to != c)
             def _():
@@ -389,44 +453,57 @@
 
         return 0
 
-    lax.fori_loop(0, NY, combine, 0)
+    def on_to_planes(i):
+        row = (y + 2 * NY - 1 - i) % NY
+        for n in range(NX):
+            src = row * NX + n
+
+            @pl.when(src != c)
+            def _():
+                k = (c + nc - src) % nc
+                remote(outp.at[src], ob.at[src], o_s.at[k], o_r.at[k], at(src)).wait_recv()
+
+        for n in range(NX // per):
+            to = row * (NX // per) + n
+
+            @pl.when(to != j)
+            def _():
+                zo_copy(to).start()
+
+    def rows_step(i, _):
+        combine(i, 0)
+
+        @pl.when(i > 0)
+        def _():
+            on_to_planes(i - 1)
+
+        return 0
+
+    lax.fori_loop(0, NY, rows_step, 0)
     ob[c] = outp[c]
-
-    def o_wait(k, _):
-        src = (c + nc - k) % nc
-        remote(outp.at[src], ob.at[src], o_s.at[k], o_r.at[k], at(src)).wait_recv()
-        return 0
-
-    lax.fori_loop(1, nc, o_wait, 0)
-
-    def zo_copy(k):
-        to = (j + k) % n_z
-        return remote(ob.at[pl.ds(per * to, per)], zb.at[k], zo_s.at[k], zo_r.at[k], {"dp": dp, "mp": to})
-
-    def zo_start(k, _):
-        zo_copy(k).start()
-        return 0
-
-    lax.fori_loop(1, n_z, zo_start, 0)
+    on_to_planes(NY - 1)
     total = ob[pl.ds(per * j, per)].astype(F32)
     for k in range(1, n_z):
-        zo_copy(k).wait_recv()
+        from_z(k).wait_recv()
         total = total + zb[k].astype(F32)
-    mix[...] = total.astype(BF16)
-
-    own_fresh.wait()
-
-    def f_wait(k, _):
-        src = (dp + n_dp - k) % n_dp
-        remote(packed.at[src], fresh.at[src], f_s.at[k], f_r.at[k], {"dp": src, "mp": j}).wait_recv()
-        f_copy(k).wait_send()
-        return 0
-
-    lax.fori_loop(1, n_dp, f_wait, 0)
-
+    mix[...] = jnp.concatenate([total[i] for i in range(per)], axis=1).astype(BF16)
+
+    for cp in f2_own:
+        cp.wait()
+    for k, d in steps:
+        if k < NY:
+            f2_from(k, d, False).wait_recv()
+            f2_copy(k, d, False).wait_send()
+        if k < NX:
+            f2_from(k, d, True).wait_recv()
+            f2_copy(k, d, True).wait_send()
+    for k in range(1, NX):
+        f1_copy(k, False).wait_send()
+    for k in range(1, NY):
+        f1_copy(k, True).wait_send()
     def z_done(k, _):
         z_copy(k).wait_send()
-        zo_copy(k).wait_send()
+        zo_copy((j + k) % n_z).wait_send()
         return 0
 
     lax.fori_loop(1, n_z, z_done, 0)
@@ -474,8 +551,8 @@
     for m, out in enumerate((gate, up, down)):
         w = fresh[:, m].reshape(rows // BLK, BLK, BLK).astype(F32)
         top = jnp.max(jnp.max(jnp.abs(w), axis=1, keepdims=True), axis=2, keepdims=True) + EPS
-        out[0] = (w / top).astype(BF16).reshape(rows, BLK)
-        scales[0, m] = jnp.broadcast_to(top, (rows // BLK, 1, BLK)).reshape(rows // BLK, BLK)
+        out[0] = (w * (1.0 / top)).astype(BF16).reshape(rows, BLK)
+        scales[m, 0] = top.reshape(rows // BLK, 1)
 
 
 def local(tokens, expert_ids, route_weights, placement_of, gate_weight, up_weight, down_weight):
@@ -486,14 +563,9 @@
     top = expert_ids.shape[1]
     dc, per, lanes = 2 * dr, wide // (2 * dr), NX * tg
     slots = n_e * CAP
-    h = lax.axis_index("dp") % 2
 
     order = jnp.arange(n_e, dtype=jnp.int32)
     inv = jnp.sum(jnp.where(placement_of[:, None] == order[None, :], order[:, None], 0), axis=0)
-    pieces = tokens.reshape(tg, per, 2, dr)
-    pieces = jnp.where(h == 0, pieces, pieces[:, :, ::-1]).reshape(tg, per, dc).transpose(1, 0, 2)
-    ids4 = jnp.tile(expert_ids.T, (1, NX))
-    rw4 = jnp.tile(route_weights.T, (1, NX))
 
     vm = pltpu.VMEM
     dma = pltpu.SemaphoreType.DMA
@@ -503,14 +575,17 @@
     fresh, mix = pl.pallas_call(
         routed_kernel,
         out_shape=(
-            jax.ShapeDtypeStruct((n_dp, 3, dr, BLK), BF16),
-            jax.ShapeDtypeStruct((per, tg, dc), BF16),
+            jax.ShapeDtypeStruct((NY, NX, 2, 3, dr, BLK), BF16),
+            jax.ShapeDtypeStruct((tg, wide), BF16),
         ),
         in_specs=[pl.BlockSpec(memory_space=pltpu.SMEM), vmem, vmem, vmem, hbm, hbm, hbm],
         out_specs=(hbm, vmem),
         scratch_shapes=weights
         + [
-            vm((n_dp, 3, dr, BLK), BF16),
+            vm((NY, NX, 2, 3, dr, BLK), BF16),
+            vm((NX, NY, 2, 3, dr // 2, BLK), BF16),
+            vm((NY, NX, 2, 3, dr // 2, BLK), BF16),
+            vm((per, tg, dc), BF16),
             vm((nc, top, lanes), jnp.int32),
             vm((NY, n_e, lanes), F32),
             vm((slots, BLK), F32),
@@ -528,7 +603,7 @@
             vm((nc, tg, dc), BF16),
             vm((nc, tg, dc), BF16),
             vm((n_z, per, tg, dc), BF16),
-            dma((4,)),
+            dma((6,)),
             dma((nc,)), dma((nc,)),
             dma((n_z,)), dma((n_z,)),
             dma((nc,)), dma((nc,)),
@@ -538,10 +613,12 @@
             dma((NCH, 4)), dma((NCH, 4, 4)), dma((NCH, nc)),
             dma((nc,)), dma((nc,)),
             dma((n_z,)), dma((n_z,)),
-            dma((n_dp,)), dma((n_dp,)),
+            dma((2, 3)), dma((2, 3)),
+            dma((2, 4, 2)), dma((2, 4, 2)),
         ],
         compiler_params=pltpu.CompilerParams(collective_id=0, has_side_effects=True, vmem_limit_bytes=62 * 1024 * 1024),
-    )(inv, ids4, rw4, pieces, gate_weight, up_weight, down_weight)
+    )(inv, expert_ids.T, route_weights.T, tokens, gate_weight, up_weight, down_weight)
+    fresh = fresh.reshape(n_dp, 3, dr, BLK)
 
     step = max(1, BLK // dr if dr < BLK else 4)
     rows = step * dr
@@ -551,15 +628,13 @@
     gate_q, up_q, down_q, scales = pl.pallas_call(
         quantize_kernel,
         grid=(grid,),
-        out_shape=(out_w, out_w, out_w, jax.ShapeDtypeStruct((grid, 3, rows // BLK, BLK), F32)),
+        out_shape=(out_w, out_w, out_w, jax.ShapeDtypeStruct((3, grid, rows // BLK, 1), F32)),
         in_specs=[pl.BlockSpec((step, 3, dr, BLK), lambda i: (i, 0, 0, 0))],
-        out_specs=(spec_w, spec_w, spec_w, pl.BlockSpec((1, 3, rows // BLK, BLK), lambda i: (i, 0, 0, 0))),
+        out_specs=(spec_w, spec_w, spec_w, pl.BlockSpec((3, 1, rows // BLK, 1), lambda i: (0, i, 0, 0))),
     )(fresh)
-    scales = scales[:, :, :, 0].transpose(1, 0, 2).reshape(3, 1, -1, 1)
-
-    mixed = mix.transpose(1, 0, 2).reshape(tg, per, 2, dr)
-    mixed = jnp.where(h == 0, mixed, mixed[:, :, ::-1]).reshape(tg, wide)
-    return gate_q, up_q, down_q, scales, mixed
+    scales = scales.reshape(3, 1, -1, 1)
+
+    return gate_q, up_q, down_q, scales, mix
 
 
 def solution(mesh):

time: 262 us -> 214 us (0.82)
  the two profiles are of different devices: /device:TPU:24 before, /device:TPU:32 now
where the time goes in v2:
time: 214 us
  Pallas kernels  210 us (98%)
  other arithmetic  2.24 us (1%)
    pallas_call x1, Pallas kernels, local(): pl.pallas_call(routed_kernel, out_shape=(jax.ShapeDtypeStruct((NY, NX, 2,...  202 us
    pallas_call x1, Pallas kernels, local(): pl.pallas_call(quantize_kernel, grid=(grid,), out_shape=(out_w, out_w, ou...  7.88 us

profile of v2, /device:TPU:32, one launch (start us, length us, event | category | flops | bytes accessed | tf_op | source)
XLA Modules:
  0.0 213.8 jit_solution(3302360149897147308)
XLA Ops:
  0.6 1.3 select_reduce_fusion.inv
  1.9 201.7 %shard_map.110 = (bf16[4,4,2,3,224,128]{5,4,3,2,1,0:T(8,128)(2,1)}, bf16[64,896]{1,0:T(8,128)(2,1)}) custom-call(s32[32]{0:T(128)} %select_reduce_fusion.inv, s32[8,64]{1,0:T(8,128)} %bitcast.5, f32[8,64]{1,0:T(8,128)} %bitcast.6, bf16[64,896]{1,0:T(8,128)(2,1)} %tok.1, bf16[32,224,128]{2,1,0:T(8,128)(2,1)} %wg.1, bf16[32,224,128]{2,1,0:T(8,128)(2,1)} %wu.1, ...), custom_call_target="tpu_custom_call" | custom-call | tf_op jit(solution)/shard_map/pallas_call | solution.py:575
  203.6 0.0 copy-start
  203.6 7.9 %shard_map.111 = (bf16[1,7168,128]{2,1,0:T(8,128)(2,1)}, bf16[1,7168,128]{2,1,0:T(8,128)(2,1)}, bf16[1,7168,128]{2,1,0:T(8,128)(2,1)}, f32[3,8,7,1]{3,2,1,0:T(8,128)}) custom-call(bf16[32,3,224,128]{3,2,1,0:T(8,128)(2,1)} %bitcast.4), custom_call_target="tpu_custom_call" | custom-call | tf_op jit(solution)/shard_map/pallas_call | solution.py:628
  211.5 1.0 reduce
  212.5 0.6 reshape.18
  213.2 0.0 copy-done
  213.2 0.6 copy.16
Async XLA Ops:
  203.6 9.5 %copy-start = (bf16[64,896]{1,0:T(8,128)(2,1)S(1)}, bf16[64,896]{1,0:T(8,128)(2,1)}, u32[]{:S(2)}) copy-start(bf16[64,896]{1,0:T(8,128)(2,1)} %get-tuple-element.41) | copy-start | bytes 344068

commit v3 on v2

--- a/solution.py
+++ b/solution.py
@@ -18,10 +18,10 @@
 def routed_kernel(
     inv, ids, rw, tok, wg, wu, wd,
     fresh, mix,
-    wog, wou, wod, wsg, wsu, wsd, packed, st_a, st_b, tokp, ids_all, pos_all, slot_w, tz, xs, xg, part,
-    rg, ru, qg, qu, r2g, r2u, hid, outp, ob, zb,
-    loc, ids_s, ids_r, z_s, z_r, t_s, t_r, w_s, w_r, r1_s, r1_r, r2_s, r2_r, a1_s, a2_s, a_r,
-    o_s, o_r, zo_s, zo_r, f1_s, f1_r, f2_s, f2_r,
+    wog, wou, wod, wsg, wsu, wsd, packed, st_a, st_b, tokp, ids_all, pos_all, slot_w, xs, xg, part,
+    hg, hu, rg, ru, qg, qu, r2g, r2u, hid, outp, zb, fin, ob,
+    loc, ids_s, ids_r, z_s, z_r, t_s, t_r, w_s, w_r, r0_s, r0_r, r1_s, r1_r, r2_s, r2_r,
+    a1_s, a1_r, a2_s, a2_r, a3_s, a3_r, zo_s, zo_r, m_s, m_r, f1_s, f1_r, f2_s, f2_r,
 ):
     dp, j = lax.axis_index("dp"), lax.axis_index("mp")
     n_dp, n_z = lax.axis_size("dp"), lax.axis_size("mp")
@@ -30,7 +30,8 @@
     y, x = c // NX, c % NX
     sib = 2 * c + 1 - h
     n_e, dr, _ = wog.shape
-    per = tz.shape[0] // n_z
+    per = nc // n_z
+    home = c // per
     top, tg = ids.shape
     lanes = NX * tg
     eb = n_e // NCH
@@ -49,8 +50,6 @@
         cp.start()
     for i in range(per):
         tokp[i] = tok[:, i * dc : (i + 1) * dc]
-    own_tok = pltpu.make_async_copy(tokp, tz.at[pl.ds(per * j, per)], loc.at[3])
-    own_tok.start()
 
     lane_g = sum([(lax.broadcasted_iota(jnp.int32, (1, lanes), 1) >= i * tg).astype(jnp.int32) for i in range(1, NX)], jnp.zeros((1, lanes), jnp.int32))
     mine = jnp.where(lane_g == x, jnp.concatenate([ids[...]] * NX, axis=1), -1)
@@ -69,17 +68,29 @@
         return 0
 
     lax.fori_loop(1, n_z, greet_z, 0)
-    pl.semaphore_wait(barrier, n_dp + n_z - 2)
-
-    def z_copy(k):
-        to = (j + k) % n_z
-        return remote(tokp, tz.at[pl.ds(per * j, per)], z_s.at[k], z_r.at[k], {"dp": dp, "mp": to})
-
-    def z_start(k, _):
-        z_copy(k).start()
-        return 0
-
-    lax.fori_loop(1, n_z, z_start, 0)
+    for i in range(per):
+
+        @pl.when(per * j + i != c)
+        def _():
+            pl.semaphore_signal(barrier, inc=1, device_id={"dp": 2 * (per * j + i) + h, "mp": home}, device_id_type=MESH)
+
+    pl.semaphore_wait(barrier, n_dp + n_z - 2 + per - jnp.where(home == j, 1, 0))
+
+    def t_copy(i):
+        return remote(tokp.at[i], xs.at[c], t_s.at[i], t_r.at[c % per], {"dp": 2 * (per * j + i) + h, "mp": home})
+
+    def t_from(i):
+        return remote(tokp.at[i], xs.at[per * j + i], t_s.at[i], t_r.at[i], {"dp": 2 * (per * j + i) + h, "mp": home})
+
+    for i in range(per):
+
+        @pl.when(per * j + i != c)
+        def _():
+            t_copy(i).start()
+
+    @pl.when(home == j)
+    def _():
+        xs[c] = tokp[c % per]
 
     def ids_copy(k):
         return remote(ids_all.at[c], ids_all.at[c], ids_s.at[k], ids_r.at[k], at((c + k) % nc))
@@ -193,26 +204,28 @@
         ws = jnp.sum(jnp.where(pe == p_iota[None], we, 0.0), axis=2, keepdims=True)
         slot_w[q * rows_ch : (q + 1) * rows_ch, :] = jnp.broadcast_to(ws.reshape(rows_ch, 1), (rows_ch, BLK))
 
-    own_tok.wait()
+    def z_copy(k):
+        to = (j + k) % n_z
+        held = xs.at[pl.ds(per * j, per)]
+        return remote(held, held, z_s.at[k], z_r.at[k], {"dp": dp, "mp": to})
+
+    def z_start(k, _):
+        z_copy(k).start()
+        return 0
 
     def z_wait(k, _):
         src = (j + n_z - k) % n_z
-        remote(tokp, tz.at[pl.ds(per * src, per)], z_s.at[k], z_r.at[k], {"dp": dp, "mp": src}).wait_recv()
-        return 0
-
-    lax.fori_loop(1, n_z, z_wait, 0)
-
-    def t_copy(k):
-        to = (c + k) % nc
-        return remote(tz.at[to], xs.at[c], t_s.at[k], t_r.at[k], at(to))
-
-    def t_start(k, _):
-        t_copy(k).start()
-        return 0
-
-    lax.fori_loop(1, nc, t_start, 0)
-    own_x = pltpu.make_async_copy(tz.at[c], xs.at[c], loc.at[3])
-    own_x.start()
+        held = xs.at[pl.ds(per * src, per)]
+        remote(held, held, z_s.at[k], z_r.at[k], {"dp": dp, "mp": src}).wait_recv()
+        return 0
+
+    for i in range(per):
+
+        @pl.when(per * j + i != c)
+        def _():
+            t_from(i).wait_recv()
+
+    lax.fori_loop(1, n_z, z_start, 0)
 
     def ids_wait(k, _):
         src = (c + nc - k) % nc
@@ -229,14 +242,7 @@
         return 0
 
     lax.fori_loop(0, NY, place, 0)
-    own_x.wait()
-
-    def t_wait(k, _):
-        src = (c + nc - k) % nc
-        remote(tz.at[src], xs.at[src], t_s.at[k], t_r.at[k], at(src)).wait_recv()
-        return 0
-
-    lax.fori_loop(1, nc, t_wait, 0)
+    lax.fori_loop(1, n_z, z_wait, 0)
     for cp in sib_w:
         cp.wait_recv()
 
@@ -275,12 +281,45 @@
     def rows_of(q):
         return pl.ds(pl.multiple_of(q * rows_ch, rows_ch), rows_ch)
 
-    def r1_copy(q, k, up):
+    hy, hx = NY // 2, NX // 2
+
+    def near(way, up):
         if up:
-            to = (y + k) % NY
-            return remote(part.at[to, :, rows_of(q), pl.ds(BLK, BLK)], ru.at[k - 1, :, rows_of(q), :], r1_s.at[1, q, k - 1], r1_r.at[1, q, k - 1], at(to * NX + x))
-        to = (x + k) % NX
-        return remote(part.at[:, to, rows_of(q), pl.ds(0, BLK)], rg.at[k - 1, :, rows_of(q), :], r1_s.at[0, q, k - 1], r1_r.at[0, q, k - 1], at(y * NX + to))
+            return (y + 1) % NY if way == 0 else (y + NY - 1) % NY
+        return (x + 1) % NX if way == 0 else (x + NX - 1) % NX
+
+    def chip_near(way, up):
+        return near(way, up) * NX + x if up else y * NX + near(way, up)
+
+    def r0_copy(q, way, up):
+        if up:
+            src, dst = part.at[(y + 2) % NY, pl.ds(way * hx, hx), rows_of(q), pl.ds(BLK, BLK)], hu
+        else:
+            src, dst = part.at[pl.ds(way * hy, hy), (x + 2) % NX, rows_of(q), pl.ds(0, BLK)], hg
+        u = int(up)
+        return remote(src, dst.at[way, :, rows_of(q), :], r0_s.at[u, q, way], r0_r.at[u, q, way], at(chip_near(way, up)))
+
+    def r1_copy(q, way, up):
+        if up:
+            src, dst = part.at[near(way, up), :, rows_of(q), pl.ds(BLK, BLK)], ru
+        else:
+            src, dst = part.at[:, near(way, up), rows_of(q), pl.ds(0, BLK)], rg
+        u = int(up)
+        return remote(src, dst.at[way, :, rows_of(q), :], r1_s.at[u, q, way], r1_r.at[u, q, way], at(chip_near(way, up)))
+
+    def pass_on(q):
+        rows = rows_of(q)
+        for way in range(2):
+            r0_copy(q, way, False).wait_recv()
+            half_y = pl.ds(way * hy, hy)
+            got = part[half_y, near(way, False), rows, pl.ds(0, BLK)].astype(F32) + hg[way, :, rows, :].astype(F32)
+            part[half_y, near(way, False), rows, pl.ds(0, BLK)] = got.astype(BF16)
+            r1_copy(q, way, False).start()
+            r0_copy(q, way, True).wait_recv()
+            half_x = pl.ds(way * hx, hx)
+            got = part[near(way, True), half_x, rows, pl.ds(BLK, BLK)].astype(F32) + hu[way, :, rows, :].astype(F32)
+            part[near(way, True), half_x, rows, pl.ds(BLK, BLK)] = got.astype(BF16)
+            r1_copy(q, way, True).start()
 
     def first(q, _):
         for b in range(NY):
@@ -293,13 +332,18 @@
             return 0
 
         lax.fori_loop(0, eb // 2, pair, 0)
-        for k in range(1, NX):
-            r1_copy(q, k, False).start()
-        for k in range(1, NY):
-            r1_copy(q, k, True).start()
+        for way in range(2):
+            r0_copy(q, way, False).start()
+            r0_copy(q, way, True).start()
+
+        @pl.when(q > 0)
+        def _():
+            pass_on(q - 1)
+
         return 0
 
     lax.fori_loop(0, NCH, first, 0)
+    pass_on(NCH - 1)
 
     def r2_copy(q, k, up):
         if up:
@@ -310,26 +354,26 @@
 
     def second(q, _):
         rows = rows_of(q)
-        for k in range(1, NX):
-            r1_copy(q, k, False).wait_recv()
+        for way in range(2):
+            r1_copy(q, way, False).wait_recv()
 
         def sum_g(i, _):
             t = part[i, x, rows, pl.ds(0, BLK)].astype(F32)
-            for k in range(NX - 1):
-                t = t + rg[k, i, rows, :].astype(F32)
+            for way in range(2):
+                t = t + rg[way, i, rows, :].astype(F32)
             qg[i, rows, :] = t.astype(BF16)
             return 0
 
         lax.fori_loop(0, NY, sum_g, 0)
         for k in range(1, NY):
             r2_copy(q, k, False).start()
-        for k in range(1, NY):
-            r1_copy(q, k, True).wait_recv()
+        for way in range(2):
+            r1_copy(q, way, True).wait_recv()
 
         def sum_u(i, _):
             t = part[y, i, rows, pl.ds(BLK, BLK)].astype(F32)
-            for k in range(NY - 1):
-                t = t + ru[k, i, rows, :].astype(F32)
+            for way in range(2):
+                t = t + ru[way, i, rows, :].astype(F32)
             qu[i, rows, :] = t.astype(BF16)
             return 0
 
@@ -345,12 +389,39 @@
             return y * NX + (x + k) % NX
         return ((y + k) % NY) * NX + x
 
-    def a_copy(q, src, dev, ss):
+    def a1_copy(q, k, along_x):
+        sl = hid.at[y, x, rows_of(q), :]
+        return remote(sl, sl, a1_s.at[q, k], a1_r.at[q, k], at(line(along_x, k)))
+
+    def a1_from(q, k, along_x):
+        src = line(along_x, (NX if along_x else NY) - k)
         sl = hid.at[src // NX, src % NX, rows_of(q), :]
-        return remote(sl, sl, ss, a_r.at[q, src], dev)
+        return remote(sl, sl, a1_s.at[q, k], a1_r.at[q, k], at(src))
+
+    def row_block(along_x, place, rows):
+        return hid.at[place, :, rows, :] if along_x else hid.at[:, place, rows, :]
+
+    def a2_copy(q, way, along_x):
+        sl = row_block(along_x, y if along_x else x, rows_of(q))
+        return remote(sl, sl, a2_s.at[q, way], a2_r.at[q, way], at(chip_near(way, along_x)))
+
+    def a2_from(q, way, along_x):
+        sl = row_block(along_x, near(1 - way, along_x), rows_of(q))
+        return remote(sl, sl, a2_s.at[q, way], a2_r.at[q, way], at(chip_near(1 - way, along_x)))
+
+    def half_rows(q, way):
+        return pl.ds(pl.multiple_of(q * rows_ch + way * (rows_ch // 2), rows_ch // 2), rows_ch // 2)
+
+    def a3_copy(q, way, along_x):
+        sl = row_block(along_x, near(1 - way, along_x), half_rows(q, way))
+        return remote(sl, sl, a3_s.at[q, way], a3_r.at[q, way], at(chip_near(way, along_x)))
+
+    def a3_from(q, way, along_x):
+        sl = row_block(along_x, (y + 2) % NY if along_x else (x + 2) % NX, half_rows(q, way))
+        return remote(sl, sl, a3_s.at[q, way], a3_r.at[q, way], at(chip_near(1 - way, along_x)))
 
     def third(along_x):
-        n1, n2 = (NX, NY) if along_x else (NY, NX)
+        n1 = NX if along_x else NY
 
         def body(q, _):
             rows = rows_of(q)
@@ -367,9 +438,7 @@
             value = gate / (1.0 + jnp.exp(-gate)) * up * slot_w[rows, :]
             hid[y, x, rows, :] = value.astype(BF16)
             for k in range(1, n1):
-                a_copy(q, c, at(line(along_x, k)), a1_s.at[q, k]).start()
-            for k in range(1, n2):
-                a_copy(q, c, at(line(not along_x, k)), a2_s.at[q, 0, k]).start()
+                a1_copy(q, k, along_x).start()
             return 0
 
         return body
@@ -378,34 +447,35 @@
     lax.fori_loop(0, half, third(True), 0)
     lax.fori_loop(half, NCH, third(False), 0)
 
+    def spread(along_x):
+        def body(q, _):
+            for k in range(1, NX if along_x else NY):
+                a1_from(q, k, along_x).wait_recv()
+            for way in range(2):
+                a2_copy(q, way, along_x).start()
+            return 0
+
+        return body
+
     def forward(along_x):
-        n1, n2 = (NX, NY) if along_x else (NY, NX)
-
         def body(q, _):
-            for k in range(1, n1):
-                src = line(along_x, n1 - k)
-                a_copy(q, src, at(src), a1_s.at[q, k]).wait_recv()
-                for m in range(1, n2):
-                    a_copy(q, src, at(line(not along_x, m)), a2_s.at[q, k, m]).start()
+            for way in range(2):
+                a2_from(q, way, along_x).wait_recv()
+                a3_copy(q, way, along_x).start()
             return 0
 
         return body
 
+    lax.fori_loop(0, half, spread(True), 0)
+    lax.fori_loop(half, NCH, spread(False), 0)
     lax.fori_loop(0, half, forward(True), 0)
     lax.fori_loop(half, NCH, forward(False), 0)
     f2_start(range(EARLY, max(NX, NY)))
 
     def down(along_x):
-        n1, n2 = (NX, NY) if along_x else (NY, NX)
-
         def body(q, _):
-            for m in range(1, n2):
-                for k in range(n1):
-                    if along_x:
-                        src = ((y + m) % NY) * NX + (x + k) % NX
-                    else:
-                        src = ((y + k) % NY) * NX + (x + m) % NX
-                    a_copy(q, src, at(src), a1_s.at[q, 0]).wait_recv()
+            for way in range(2):
+                a3_from(q, way, along_x).wait_recv()
 
             def pair(i, _):
                 e = q * eb + 2 * i
@@ -425,68 +495,62 @@
     lax.fori_loop(0, half, down(True), 0)
     lax.fori_loop(half, NCH, down(False), 0)
 
-    def o_copy(to):
-        k = (to + nc - c) % nc
-        return remote(outp.at[to], ob.at[c], o_s.at[k], o_r.at[k], at(to))
+    per_row = NX // per
 
     def zo_copy(to):
         k = (to + n_z - j) % n_z
-        return remote(ob.at[pl.ds(per * to, per)], zb.at[k], zo_s.at[k], zo_r.at[k], {"dp": dp, "mp": to})
+        return remote(outp.at[pl.ds(per * to, per)], zb.at[k], zo_s.at[k], zo_r.at[k], {"dp": dp, "mp": to})
 
     def from_z(k):
         src = (j + n_z - k) % n_z
-        return remote(ob.at[pl.ds(per * src, per)], zb.at[k], zo_s.at[k], zo_r.at[k], {"dp": dp, "mp": src})
+        return remote(outp.at[pl.ds(per * src, per)], zb.at[k], zo_s.at[k], zo_r.at[k], {"dp": dp, "mp": src})
 
     def combine(i, _):
-        b = (y + 1 + i) % NY
+        b = (j // per_row + 1 + i) % NY
         total = jnp.zeros((lanes, dc), F32)
         for q in range(NCH):
             d = xg[pl.ds(q * eb, eb), b].reshape(eb * NX * CAP, dc)
             total = total + lax.dot_general(one_hot(b, q), d, (((0,), (0,)), ((), ())), preferred_element_type=F32)
         outp[pl.ds(b * NX, NX)] = total.astype(BF16).reshape(NX, tg, dc)
-        for n in range(NX):
-            to = b * NX + n
-
-            @pl.when(to != c)
-            def _():
-                o_copy(to).start()
-
-        return 0
-
-    def on_to_planes(i):
-        row = (y + 2 * NY - 1 - i) % NY
-        for n in range(NX):
-            src = row * NX + n
-
-            @pl.when(src != c)
-            def _():
-                k = (c + nc - src) % nc
-                remote(outp.at[src], ob.at[src], o_s.at[k], o_r.at[k], at(src)).wait_recv()
-
-        for n in range(NX // per):
-            to = row * (NX // per) + n
+        for n in range(per_row):
+            to = b * per_row + n
 
             @pl.when(to != j)
             def _():
                 zo_copy(to).start()
 
-    def rows_step(i, _):
-        combine(i, 0)
-
-        @pl.when(i > 0)
-        def _():
-            on_to_planes(i - 1)
-
-        return 0
-
-    lax.fori_loop(0, NY, rows_step, 0)
-    ob[c] = outp[c]
-    on_to_planes(NY - 1)
-    total = ob[pl.ds(per * j, per)].astype(F32)
+        return 0
+
+    lax.fori_loop(0, NY, combine, 0)
+    total = outp[pl.ds(per * j, per)].astype(F32)
     for k in range(1, n_z):
         from_z(k).wait_recv()
         total = total + zb[k].astype(F32)
-    mix[...] = jnp.concatenate([total[i] for i in range(per)], axis=1).astype(BF16)
+    fin[...] = total.astype(BF16)
+
+    def m_copy(i):
+        return remote(fin.at[i], ob.at[c % per], m_s.at[i], m_r.at[c % per], {"dp": 2 * (per * j + i) + h, "mp": home})
+
+    def m_from(i):
+        return remote(fin.at[i], ob.at[i], m_s.at[i], m_r.at[i], {"dp": 2 * (per * j + i) + h, "mp": home})
+
+    for i in range(per):
+
+        @pl.when(per * j + i != c)
+        def _():
+            m_copy(i).start()
+
+    @pl.when(home == j)
+    def _():
+        ob[c % per] = fin[c % per]
+
+    for i in range(per):
+
+        @pl.when(per * j + i != c)
+        def _():
+            m_from(i).wait_recv()
+
+    mix[...] = jnp.concatenate([ob[i] for i in range(per)], axis=1)
 
     for cp in f2_own:
         cp.wait()
@@ -507,11 +571,15 @@
         return 0
 
     lax.fori_loop(1, n_z, z_done, 0)
+    for i in range(per):
+
+        @pl.when(per * j + i != c)
+        def _():
+            t_copy(i).wait_send()
+            m_copy(i).wait_send()
 
     def plane_done(k, _):
         ids_copy(k).wait_send()
-        t_copy(k).wait_send()
-        o_copy((c + k) % nc).wait_send()
         return 0
 
     lax.fori_loop(1, nc, plane_done, 0)
@@ -519,25 +587,25 @@
         cp.wait_send()
 
     def sums_done(q, _):
+        for way in range(2):
+            for up in (False, True):
+                r0_copy(q, way, up).wait_send()
+                r1_copy(q, way, up).wait_send()
         for k in range(1, NX):
-            r1_copy(q, k, False).wait_send()
             r2_copy(q, k, True).wait_send()
         for k in range(1, NY):
-            r1_copy(q, k, True).wait_send()
             r2_copy(q, k, False).wait_send()
         return 0
 
     lax.fori_loop(0, NCH, sums_done, 0)
 
     def hid_done(along_x):
-        n1, n2 = (NX, NY) if along_x else (NY, NX)
-
         def body(q, _):
-            for k in range(1, n1):
-                a_copy(q, c, at(c), a1_s.at[q, k]).wait_send()
-            for k in range(n1):
-                for m in range(1, n2):
-                    a_copy(q, c, at(c), a2_s.at[q, k, m]).wait_send()
+            for k in range(1, NX if along_x else NY):
+                a1_copy(q, k, along_x).wait_send()
+            for way in range(2):
+                a2_copy(q, way, along_x).wait_send()
+                a3_copy(q, way, along_x).wait_send()
             return 0
 
         return body
@@ -549,9 +617,9 @@
 def quantize_kernel(fresh, gate, up, down, scales):
     rows = gate.shape[1]
     for m, out in enumerate((gate, up, down)):
-        w = fresh[:, m].reshape(rows // BLK, BLK, BLK).astype(F32)
-        top = jnp.max(jnp.max(jnp.abs(w), axis=1, keepdims=True), axis=2, keepdims=True) + EPS
-        out[0] = (w * (1.0 / top)).astype(BF16).reshape(rows, BLK)
+        w = fresh[:, m].reshape(rows // BLK, BLK, BLK)
+        top = jnp.max(jnp.max(jnp.abs(w), axis=1, keepdims=True).astype(F32), axis=2, keepdims=True) + EPS
+        out[0] = (w.astype(F32) * (1.0 / top)).astype(BF16).reshape(rows, BLK)
         scales[m, 0] = top.reshape(rows // BLK, 1)
 
 
@@ -590,29 +658,34 @@
             vm((NY, n_e, lanes), F32),
             vm((slots, BLK), F32),
             vm((nc, tg, dc), BF16),
-            vm((nc, tg, dc), BF16),
             vm((n_e, NY, NX * CAP, dc), BF16),
             vm((NY, NX, slots, 2 * BLK), BF16),
-            vm((NX - 1, NY, slots, BLK), BF16),
-            vm((NY - 1, NX, slots, BLK), BF16),
+            vm((2, NY // 2, slots, BLK), BF16),
+            vm((2, NX // 2, slots, BLK), BF16),
+            vm((2, NY, slots, BLK), BF16),
+            vm((2, NX, slots, BLK), BF16),
             vm((NY, slots, BLK), BF16),
             vm((NX, slots, BLK), BF16),
             vm((NY - 1, slots, BLK), BF16),
             vm((NX - 1, slots, BLK), BF16),
             vm((NY, NX, slots, BLK), BF16),
             vm((nc, tg, dc), BF16),
-            vm((nc, tg, dc), BF16),
             vm((n_z, per, tg, dc), BF16),
+            vm((per, tg, dc), BF16),
+            vm((per, tg, dc), BF16),
             dma((6,)),
             dma((nc,)), dma((nc,)),
             dma((n_z,)), dma((n_z,)),
-            dma((nc,)), dma((nc,)),
+            dma((per,)), dma((per,)),
             dma((3,)), dma((3,)),
+            dma((2, NCH, 2)), dma((2, NCH, 2)),
+            dma((2, NCH, 2)), dma((2, NCH, 2)),
             dma((2, NCH, 3)), dma((2, NCH, 3)),
-            dma((2, NCH, 3)), dma((2, NCH, 3)),
-            dma((NCH, 4)), dma((NCH, 4, 4)), dma((NCH, nc)),
-            dma((nc,)), dma((nc,)),
+            dma((NCH, 4)), dma((NCH, 4)),
+            dma((NCH, 2)), dma((NCH, 2)),
+            dma((NCH, 2)), dma((NCH, 2)),
             dma((n_z,)), dma((n_z,)),
+            dma((per,)), dma((per,)),
             dma((2, 3)), dma((2, 3)),
             dma((2, 4, 2)), dma((2, 4, 2)),
         ],

time: 214 us -> 175 us (0.82)
  the two profiles are of different devices: /device:TPU:32 before, /device:TPU:10 now
where the time goes in v3:
time: 175 us; the launch traced here: 174 us
  Pallas kernels  170 us (97%)
  other arithmetic  2.24 us (1%)
    pallas_call x1, Pallas kernels, local(): pl.pallas_call(routed_kernel, out_shape=(jax.ShapeDtypeStruct((NY, NX, 2,...  162 us
    pallas_call x1, Pallas kernels, local(): pl.pallas_call(quantize_kernel, grid=(grid,), out_shape=(out_w, out_w, ou...  8.08 us

profile of v3, /device:TPU:10, one launch (start us, length us, event | category | flops | bytes accessed | tf_op | source)
XLA Modules:
  0.0 174.4 jit_solution(2328211658584710903)
XLA Ops:
  0.6 1.3 select_reduce_fusion.inv
  1.9 162.2 %shard_map.110 = (bf16[4,4,2,3,224,128]{5,4,3,2,1,0:T(8,128)(2,1)}, bf16[64,896]{1,0:T(8,128)(2,1)}) custom-call(s32[32]{0:T(128)} %select_reduce_fusion.inv, s32[8,64]{1,0:T(8,128)} %bitcast.5, f32[8,64]{1,0:T(8,128)} %bitcast.6, bf16[64,896]{1,0:T(8,128)(2,1)} %tok.1, bf16[32,224,128]{2,1,0:T(8,128)(2,1)} %wg.1, bf16[32,224,128]{2,1,0:T(8,128)(2,1)} %wu.1, ...), custom_call_target="tpu_custom_call" | custom-call | tf_op jit(solution)/shard_map/pallas_call | solution.py:643
  164.1 0.0 copy-start
  164.1 8.1 %shard_map.111 = (bf16[1,7168,128]{2,1,0:T(8,128)(2,1)}, bf16[1,7168,128]{2,1,0:T(8,128)(2,1)}, bf16[1,7168,128]{2,1,0:T(8,128)(2,1)}, f32[3,8,7,1]{3,2,1,0:T(8,128)}) custom-call(bf16[32,3,224,128]{3,2,1,0:T(8,128)(2,1)} %bitcast.4), custom_call_target="tpu_custom_call" | custom-call | tf_op jit(solution)/shard_map/pallas_call | solution.py:701
  172.1 1.0 reduce
  173.1 0.6 reshape.18
  173.8 0.0 copy-done
  173.8 0.6 copy.16
Async XLA Ops:
  164.1 9.7 %copy-start = (bf16[64,896]{1,0:T(8,128)(2,1)S(1)}, bf16[64,896]{1,0:T(8,128)(2,1)}, u32[]{:S(2)}) copy-start(bf16[64,896]{1,0:T(8,128)(2,1)} %get-tuple-element.41) | copy-start | bytes 344068

commit v4 on v3

--- a/solution.py
+++ b/solution.py
@@ -10,7 +10,7 @@
 EPS = 1e-06
 NY, NX = 4, 4
 NCH = 4
-EARLY = 1
+REST = NCH + 4
 MESH = pl.DeviceIdType.MESH
 F32, BF16 = jnp.float32, jnp.bfloat16
 
@@ -18,7 +18,7 @@
 def routed_kernel(
     inv, ids, rw, tok, wg, wu, wd,
     fresh, mix,
-    wog, wou, wod, wsg, wsu, wsd, packed, st_a, st_b, tokp, ids_all, pos_all, slot_w, xs, xg, part,
+    wog, wou, wod, wsg, wsu, wsd, packed, st_a, st_b, tokp, ids_all, pos_all, hots, slot_w, xs, xg, part,
     hg, hu, rg, ru, qg, qu, r2g, r2u, hid, outp, zb, fin, ob,
     loc, ids_s, ids_r, z_s, z_r, t_s, t_r, w_s, w_r, r0_s, r0_r, r1_s, r1_r, r2_s, r2_r,
     a1_s, a1_r, a2_s, a2_r, a3_s, a3_r, zo_s, zo_r, m_s, m_r, f1_s, f1_r, f2_s, f2_r,
@@ -74,6 +74,18 @@
         def _():
             pl.semaphore_signal(barrier, inc=1, device_id={"dp": 2 * (per * j + i) + h, "mp": home}, device_id_type=MESH)
 
+    for cp in own_w:
+        cp.wait()
+
+    def pack(s, _):
+        e = inv[s]
+        to = (s // (2 * NX), (s // 2) % NX, s % 2)
+        packed[to[0], to[1], to[2], 0] = wog[e]
+        packed[to[0], to[1], to[2], 1] = wou[e]
+        packed[to[0], to[1], to[2], 2] = wod[e]
+        return 0
+
+    lax.fori_loop(0, n_e, pack, 0)
     pl.semaphore_wait(barrier, n_dp + n_z - 2 + per - jnp.where(home == j, 1, 0))
 
     def t_copy(i):
@@ -107,18 +119,6 @@
     for cp in sib_w:
         cp.start()
 
-    for cp in own_w:
-        cp.wait()
-
-    def pack(s, _):
-        e = inv[s]
-        to = (s // (2 * NX), (s // 2) % NX, s % 2)
-        packed[to[0], to[1], to[2], 0] = wog[e]
-        packed[to[0], to[1], to[2], 1] = wou[e]
-        packed[to[0], to[1], to[2], 2] = wod[e]
-        return 0
-
-    lax.fori_loop(0, n_e, pack, 0)
     hr = dr // 2
     top_rows, low_rows = pl.ds(0, hr), pl.ds(hr, hr)
 
@@ -204,20 +204,20 @@
         ws = jnp.sum(jnp.where(pe == p_iota[None], we, 0.0), axis=2, keepdims=True)
         slot_w[q * rows_ch : (q + 1) * rows_ch, :] = jnp.broadcast_to(ws.reshape(rows_ch, 1), (rows_ch, BLK))
 
-    def z_copy(k):
-        to = (j + k) % n_z
-        held = xs.at[pl.ds(per * j, per)]
-        return remote(held, held, z_s.at[k], z_r.at[k], {"dp": dp, "mp": to})
-
-    def z_start(k, _):
-        z_copy(k).start()
-        return 0
-
-    def z_wait(k, _):
-        src = (j + n_z - k) % n_z
-        held = xs.at[pl.ds(per * src, per)]
-        remote(held, held, z_s.at[k], z_r.at[k], {"dp": dp, "mp": src}).wait_recv()
-        return 0
+    far = n_z // 2
+    hp = per // 2
+
+    def z_copy(s, way):
+        src = (j + n_z - s) % n_z if way == 0 else (j + s) % n_z
+        to = (j + 1) % n_z if way == 0 else (j + n_z - 1) % n_z
+        held = xs.at[pl.ds(per * src + way * hp, hp)] if s == far - 1 else xs.at[pl.ds(per * src, per)]
+        return remote(held, held, z_s.at[way, s], z_r.at[way, s], {"dp": dp, "mp": to})
+
+    def z_from(s, way):
+        src = (j + n_z - s - 1) % n_z if way == 0 else (j + s + 1) % n_z
+        to = (j + n_z - 1) % n_z if way == 0 else (j + 1) % n_z
+        held = xs.at[pl.ds(per * src + way * hp, hp)] if s == far - 1 else xs.at[pl.ds(per * src, per)]
+        return remote(held, held, z_s.at[way, s], z_r.at[way, s], {"dp": dp, "mp": to})
 
     for i in range(per):
 
@@ -225,7 +225,8 @@
         def _():
             t_from(i).wait_recv()
 
-    lax.fori_loop(1, n_z, z_start, 0)
+    for way in range(2):
+        z_copy(0, way).start()
 
     def ids_wait(k, _):
         src = (c + nc - k) % nc
@@ -233,41 +234,38 @@
         return 0
 
     lax.fori_loop(1, nc, ids_wait, 0)
+
+    r_iota = lax.broadcasted_iota(jnp.int32, (NX * CAP, lanes), 0)
+    r_of = sum([(r_iota >= i * CAP).astype(jnp.int32) for i in range(1, NX)], jnp.zeros((NX * CAP, lanes), jnp.int32))
+    want = jnp.where(r_of == lane_g, r_iota - CAP * r_of, -9).astype(F32)
 
     def place(b, _):
         ids = ids_all[b * NX]
         for i in range(1, NX):
             ids = jnp.maximum(ids, ids_all[b * NX + i])
         pos_all[b] = positions(ids)
-        return 0
-
-    lax.fori_loop(0, NY, place, 0)
-    lax.fori_loop(1, n_z, z_wait, 0)
+
+        def hot(q, _):
+            pe = pos_all[b, pl.ds(pl.multiple_of(q * eb, eb), eb), :].reshape(eb, 1, lanes)
+            hots[b, q] = jnp.where(pe == want[None], 1.0, 0.0).astype(BF16).reshape(eb * NX * CAP, lanes)
+            return 0
+
+        return lax.fori_loop(0, NCH, hot, 0)
+
+    for s in range(1, far):
+        lax.fori_loop(NY * (s - 1) // (far - 1), NY * s // (far - 1), place, 0)
+        for way in range(2):
+            z_from(s - 1, way).wait_recv()
+            z_copy(s, way).start()
+    for way in range(2):
+        z_from(far - 1, way).wait_recv()
     for cp in sib_w:
         cp.wait_recv()
 
-    for cp in f1_own:
-        cp.wait()
-    for k in range(1, NX):
-        f1_from(k, False).wait_recv()
-    for k in range(1, NY):
-        f1_from(k, True).wait_recv()
-    for cp in f2_own:
-        cp.start()
-    f2_start(range(EARLY))
-
-    r_iota = lax.broadcasted_iota(jnp.int32, (NX * CAP, lanes), 0)
-    r_of = sum([(r_iota >= i * CAP).astype(jnp.int32) for i in range(1, NX)], jnp.zeros((NX * CAP, lanes), jnp.int32))
-    want = jnp.where(r_of == lane_g, r_iota - CAP * r_of, -9).astype(F32)
-
-    def one_hot(b, q):
-        pe = pos_all[b, pl.ds(pl.multiple_of(q * eb, eb), eb), :].reshape(eb, 1, lanes)
-        hot = jnp.where(pe == want[None], 1.0, 0.0).astype(BF16)
-        return hot.reshape(eb * NX * CAP, lanes)
 
     def pick(q, b):
         tokens = xs[pl.ds(b * NX, NX)].reshape(lanes, dc)
-        got = jnp.dot(one_hot(b, q), tokens, preferred_element_type=F32)
+        got = jnp.dot(hots[b, q], tokens, preferred_element_type=F32)
         xg[pl.ds(q * eb, eb), b] = got.astype(BF16).reshape(eb, NX * CAP, dc)
 
     def by_core(own, other):
@@ -321,7 +319,7 @@
             part[near(way, True), half_x, rows, pl.ds(BLK, BLK)] = got.astype(BF16)
             r1_copy(q, way, True).start()
 
-    def first(q, _):
+    def first(q):
         for b in range(NY):
             pick(q, b)
 
@@ -336,14 +334,7 @@
             r0_copy(q, way, False).start()
             r0_copy(q, way, True).start()
 
-        @pl.when(q > 0)
-        def _():
-            pass_on(q - 1)
-
-        return 0
-
-    lax.fori_loop(0, NCH, first, 0)
-    pass_on(NCH - 1)
+        return 0
 
     def r2_copy(q, k, up):
         if up:
@@ -352,7 +343,7 @@
         to = (y + k) % NY
         return remote(qg.at[to, rows_of(q), :], r2g.at[k - 1, rows_of(q), :], r2_s.at[0, q, k - 1], r2_r.at[0, q, k - 1], at(to * NX + x))
 
-    def second(q, _):
+    def second(q):
         rows = rows_of(q)
         for way in range(2):
             r1_copy(q, way, False).wait_recv()
@@ -382,151 +373,163 @@
             r2_copy(q, k, True).start()
         return 0
 
-    lax.fori_loop(0, NCH, second, 0)
 
     def line(q_along_x, k):
         if q_along_x:
             return y * NX + (x + k) % NX
         return ((y + k) % NY) * NX + x
 
+    hr_ch = rows_ch // 2
+
+    def half_of(q, along_x, part_of=None):
+        start, size = q * rows_ch + (0 if along_x else hr_ch), hr_ch
+        if part_of is not None:
+            start, size = start + part_of * (hr_ch // 2), hr_ch // 2
+        return pl.ds(pl.multiple_of(start, hr_ch // 2), size)
+
     def a1_copy(q, k, along_x):
-        sl = hid.at[y, x, rows_of(q), :]
-        return remote(sl, sl, a1_s.at[q, k], a1_r.at[q, k], at(line(along_x, k)))
+        sl = hid.at[y, x, half_of(q, along_x), :]
+        u = int(along_x)
+        return remote(sl, sl, a1_s.at[u, q, k], a1_r.at[u, q, k], at(line(along_x, k)))
 
     def a1_from(q, k, along_x):
         src = line(along_x, (NX if along_x else NY) - k)
-        sl = hid.at[src // NX, src % NX, rows_of(q), :]
-        return remote(sl, sl, a1_s.at[q, k], a1_r.at[q, k], at(src))
+        sl = hid.at[src // NX, src % NX, half_of(q, along_x), :]
+        u = int(along_x)
+        return remote(sl, sl, a1_s.at[u, q, k], a1_r.at[u, q, k], at(src))
 
     def row_block(along_x, place, rows):
         return hid.at[place, :, rows, :] if along_x else hid.at[:, place, rows, :]
 
     def a2_copy(q, way, along_x):
-        sl = row_block(along_x, y if along_x else x, rows_of(q))
-        return remote(sl, sl, a2_s.at[q, way], a2_r.at[q, way], at(chip_near(way, along_x)))
+        sl = row_block(along_x, y if along_x else x, half_of(q, along_x))
+        u = int(along_x)
+        return remote(sl, sl, a2_s.at[u, q, way], a2_r.at[u, q, way], at(chip_near(way, along_x)))
 
     def a2_from(q, way, along_x):
-        sl = row_block(along_x, near(1 - way, along_x), rows_of(q))
-        return remote(sl, sl, a2_s.at[q, way], a2_r.at[q, way], at(chip_near(1 - way, along_x)))
-
-    def half_rows(q, way):
-        return pl.ds(pl.multiple_of(q * rows_ch + way * (rows_ch // 2), rows_ch // 2), rows_ch // 2)
+        sl = row_block(along_x, near(1 - way, along_x), half_of(q, along_x))
+        u = int(along_x)
+        return remote(sl, sl, a2_s.at[u, q, way], a2_r.at[u, q, way], at(chip_near(1 - way, along_x)))
 
     def a3_copy(q, way, along_x):
-        sl = row_block(along_x, near(1 - way, along_x), half_rows(q, way))
-        return remote(sl, sl, a3_s.at[q, way], a3_r.at[q, way], at(chip_near(way, along_x)))
+        sl = row_block(along_x, near(1 - way, along_x), half_of(q, along_x, way))
+        u = int(along_x)
+        return remote(sl, sl, a3_s.at[u, q, way], a3_r.at[u, q, way], at(chip_near(way, along_x)))
 
     def a3_from(q, way, along_x):
-        sl = row_block(along_x, (y + 2) % NY if along_x else (x + 2) % NX, half_rows(q, way))
-        return remote(sl, sl, a3_s.at[q, way], a3_r.at[q, way], at(chip_near(1 - way, along_x)))
-
-    def third(along_x):
-        n1 = NX if along_x else NY
-
-        def body(q, _):
-            rows = rows_of(q)
-            for k in range(1, NY):
-                r2_copy(q, k, False).wait_recv()
-            for k in range(1, NX):
-                r2_copy(q, k, True).wait_recv()
-            gate = qg[y, rows, :].astype(F32)
-            for k in range(NY - 1):
-                gate = gate + r2g[k, rows, :].astype(F32)
-            up = qu[x, rows, :].astype(F32)
-            for k in range(NX - 1):
-                up = up + r2u[k, rows, :].astype(F32)
-            value = gate / (1.0 + jnp.exp(-gate)) * up * slot_w[rows, :]
-            hid[y, x, rows, :] = value.astype(BF16)
-            for k in range(1, n1):
-                a1_copy(q, k, along_x).start()
-            return 0
-
-        return body
-
-    half = NCH // 2
-    lax.fori_loop(0, half, third(True), 0)
-    lax.fori_loop(half, NCH, third(False), 0)
-
-    def spread(along_x):
-        def body(q, _):
+        sl = row_block(along_x, (y + 2) % NY if along_x else (x + 2) % NX, half_of(q, along_x, way))
+        u = int(along_x)
+        return remote(sl, sl, a3_s.at[u, q, way], a3_r.at[u, q, way], at(chip_near(1 - way, along_x)))
+
+    def third(q):
+        rows = rows_of(q)
+        for k in range(1, NY):
+            r2_copy(q, k, False).wait_recv()
+        for k in range(1, NX):
+            r2_copy(q, k, True).wait_recv()
+        gate = qg[y, rows, :].astype(F32)
+        for k in range(NY - 1):
+            gate = gate + r2g[k, rows, :].astype(F32)
+        up = qu[x, rows, :].astype(F32)
+        for k in range(NX - 1):
+            up = up + r2u[k, rows, :].astype(F32)
+        value = gate / (1.0 + jnp.exp(-gate)) * up * slot_w[rows, :]
+        hid[y, x, rows, :] = value.astype(BF16)
+        for k in range(1, NX):
+            a1_copy(q, k, True).start()
+        for k in range(1, NY):
+            a1_copy(q, k, False).start()
+
+    def spread(q):
+        for along_x in (True, False):
             for k in range(1, NX if along_x else NY):
                 a1_from(q, k, along_x).wait_recv()
             for way in range(2):
                 a2_copy(q, way, along_x).start()
-            return 0
-
-        return body
-
-    def forward(along_x):
-        def body(q, _):
+
+    def forward(q):
+        for along_x in (True, False):
             for way in range(2):
                 a2_from(q, way, along_x).wait_recv()
                 a3_copy(q, way, along_x).start()
-            return 0
-
-        return body
-
-    lax.fori_loop(0, half, spread(True), 0)
-    lax.fori_loop(half, NCH, spread(False), 0)
-    lax.fori_loop(0, half, forward(True), 0)
-    lax.fori_loop(half, NCH, forward(False), 0)
-    f2_start(range(EARLY, max(NX, NY)))
-
-    def down(along_x):
-        def body(q, _):
+
+    def down(q):
+        for along_x in (True, False):
             for way in range(2):
                 a3_from(q, way, along_x).wait_recv()
 
-            def pair(i, _):
-                e = q * eb + 2 * i
-                both = hid[:, :, pl.ds(pl.multiple_of(e * CAP, 2 * CAP), 2 * CAP), :].astype(F32).reshape(nc, 2 * CAP, BLK)
-                for o in range(2):
-                    a = both[:, o * CAP : (o + 1) * CAP, :].reshape(nc * CAP, BLK).astype(BF16)
-                    w = by_core(wod[e + o], wsd[e + o])
-                    got = lax.dot_general(a, w, (((1,), (1,)), ((), ())), preferred_element_type=F32)
-                    xg[e + o] = got.astype(BF16).reshape(NY, NX * CAP, dc)
-                return 0
-
-            lax.fori_loop(0, eb // 2, pair, 0)
+        def pair(i, _):
+            e = q * eb + 2 * i
+            both = hid[:, :, pl.ds(pl.multiple_of(e * CAP, 2 * CAP), 2 * CAP), :].astype(F32).reshape(nc, 2 * CAP, BLK)
+            for o in range(2):
+                a = both[:, o * CAP : (o + 1) * CAP, :].reshape(nc * CAP, BLK).astype(BF16)
+                w = by_core(wod[e + o], wsd[e + o])
+                got = lax.dot_general(a, w, (((1,), (1,)), ((), ())), preferred_element_type=F32)
+                xg[e + o] = got.astype(BF16).reshape(NY, NX * CAP, dc)
             return 0
 
-        return body
-
-    lax.fori_loop(0, half, down(True), 0)
-    lax.fori_loop(half, NCH, down(False), 0)
-
+        lax.fori_loop(0, eb // 2, pair, 0)
+
+    stages = [first]
+    stages += [pass_on, second]
+    stages += [third]
+    stages += [spread, forward, down]
+
+    def beat(t, _):
+        for n, stage in enumerate(stages):
+
+            @pl.when((t >= n) & (t < n + NCH))
+            def _():
+                stage(t - n)
+
+        @pl.when(t == REST)
+        def _():
+            for cp in f1_own:
+                cp.wait()
+            for k in range(1, NX):
+                f1_from(k, False).wait_recv()
+            for k in range(1, NY):
+                f1_from(k, True).wait_recv()
+            for cp in f2_own:
+                cp.start()
+            f2_start(range(max(NX, NY)))
+
+        return 0
+
+    lax.fori_loop(0, NCH + len(stages) - 1, beat, 0)
     per_row = NX // per
 
-    def zo_copy(to):
+    def zo_copy(to, n):
         k = (to + n_z - j) % n_z
-        return remote(outp.at[pl.ds(per * to, per)], zb.at[k], zo_s.at[k], zo_r.at[k], {"dp": dp, "mp": to})
-
-    def from_z(k):
+        return remote(outp.at[per * to + n], zb.at[n, k], zo_s.at[n, k], zo_r.at[n, k], {"dp": dp, "mp": to})
+
+    def from_z(k, n):
         src = (j + n_z - k) % n_z
-        return remote(outp.at[pl.ds(per * src, per)], zb.at[k], zo_s.at[k], zo_r.at[k], {"dp": dp, "mp": src})
+        return remote(outp.at[per * src + n], zb.at[n, k], zo_s.at[n, k], zo_r.at[n, k], {"dp": dp, "mp": src})
 
     def combine(i, _):
         b = (j // per_row + 1 + i) % NY
         total = jnp.zeros((lanes, dc), F32)
         for q in range(NCH):
             d = xg[pl.ds(q * eb, eb), b].reshape(eb * NX * CAP, dc)
-            total = total + lax.dot_general(one_hot(b, q), d, (((0,), (0,)), ((), ())), preferred_element_type=F32)
+            total = total + lax.dot_general(hots[b, q], d, (((0,), (0,)), ((), ())), preferred_element_type=F32)
         outp[pl.ds(b * NX, NX)] = total.astype(BF16).reshape(NX, tg, dc)
         for n in range(per_row):
             to = b * per_row + n
 
             @pl.when(to != j)
             def _():
-                zo_copy(to).start()
+                zo_copy(to, 0).start()
 
         return 0
 
     lax.fori_loop(0, NY, combine, 0)
-    total = outp[pl.ds(per * j, per)].astype(F32)
-    for k in range(1, n_z):
-        from_z(k).wait_recv()
-        total = total + zb[k].astype(F32)
-    fin[...] = total.astype(BF16)
+    def zo_start(k, _):
+        for n in range(1, per):
+            zo_copy((j + k) % n_z, n).start()
+        return 0
+
+    lax.fori_loop(1, n_z, zo_start, 0)
 
     def m_copy(i):
         return remote(fin.at[i], ob.at[c % per], m_s.at[i], m_r.at[c % per], {"dp": 2 * (per * j + i) + h, "mp": home})
@@ -535,6 +538,11 @@
         return remote(fin.at[i], ob.at[i], m_s.at[i], m_r.at[i], {"dp": 2 * (per * j + i) + h, "mp": home})
 
     for i in range(per):
+        total = outp[per * j + i].astype(F32)
+        for k in range(1, n_z):
+            from_z(k, i).wait_recv()
+            total = total + zb[i, k].astype(F32)
+        fin[i] = total.astype(BF16)
 
         @pl.when(per * j + i != c)
         def _():
@@ -566,11 +574,14 @@
     for k in range(1, NY):
         f1_copy(k, True).wait_send()
     def z_done(k, _):
-        z_copy(k).wait_send()
-        zo_copy((j + k) % n_z).wait_send()
+        for n in range(per):
+            zo_copy((j + k) % n_z, n).wait_send()
         return 0
 
     lax.fori_loop(1, n_z, z_done, 0)
+    for s in range(far):
+        for way in range(2):
+            z_copy(s, way).wait_send()
     for i in range(per):
 
         @pl.when(per * j + i != c)
@@ -599,27 +610,24 @@
 
     lax.fori_loop(0, NCH, sums_done, 0)
 
-    def hid_done(along_x):
-        def body(q, _):
+    def hid_done(q, _):
+        for along_x in (True, False):
             for k in range(1, NX if along_x else NY):
                 a1_copy(q, k, along_x).wait_send()
             for way in range(2):
                 a2_copy(q, way, along_x).wait_send()
                 a3_copy(q, way, along_x).wait_send()
-            return 0
-
-        return body
-
-    lax.fori_loop(0, half, hid_done(True), 0)
-    lax.fori_loop(half, NCH, hid_done(False), 0)
+        return 0
+
+    lax.fori_loop(0, NCH, hid_done, 0)
 
 
 def quantize_kernel(fresh, gate, up, down, scales):
     rows = gate.shape[1]
     for m, out in enumerate((gate, up, down)):
-        w = fresh[:, m].reshape(rows // BLK, BLK, BLK)
-        top = jnp.max(jnp.max(jnp.abs(w), axis=1, keepdims=True).astype(F32), axis=2, keepdims=True) + EPS
-        out[0] = (w.astype(F32) * (1.0 / top)).astype(BF16).reshape(rows, BLK)
+        w = fresh[:, m].reshape(rows // BLK, BLK, BLK).astype(F32)
+        top = jnp.max(jnp.max(jnp.abs(w), axis=1, keepdims=True), axis=2, keepdims=True) + EPS
+        out[0] = (w * (1.0 / top)).astype(BF16).reshape(rows, BLK)
         scales[m, 0] = top.reshape(rows // BLK, 1)
 
 
@@ -656,6 +664,7 @@
             vm((per, tg, dc), BF16),
             vm((nc, top, lanes), jnp.int32),
             vm((NY, n_e, lanes), F32),
+            vm((NY, NCH, slots // NCH * NX, lanes), BF16),
             vm((slots, BLK), F32),
             vm((nc, tg, dc), BF16),
             vm((n_e, NY, NX * CAP, dc), BF16),
@@ -670,21 +679,21 @@
             vm((NX - 1, slots, BLK), BF16),
             vm((NY, NX, slots, BLK), BF16),
             vm((nc, tg, dc), BF16),
-            vm((n_z, per, tg, dc), BF16),
+            vm((per, n_z, tg, dc), BF16),
             vm((per, tg, dc), BF16),
             vm((per, tg, dc), BF16),
             dma((6,)),
             dma((nc,)), dma((nc,)),
-            dma((n_z,)), dma((n_z,)),
+            dma((2, n_z // 2)), dma((2, n_z // 2)),
             dma((per,)), dma((per,)),
             dma((3,)), dma((3,)),
             dma((2, NCH, 2)), dma((2, NCH, 2)),
             dma((2, NCH, 2)), dma((2, NCH, 2)),
             dma((2, NCH, 3)), dma((2, NCH, 3)),
-            dma((NCH, 4)), dma((NCH, 4)),
-            dma((NCH, 2)), dma((NCH, 2)),
-            dma((NCH, 2)), dma((NCH, 2)),
-            dma((n_z,)), dma((n_z,)),
+            dma((2, NCH, 4)), dma((2, NCH, 4)),
+            dma((2, NCH, 2)), dma((2, NCH, 2)),
+            dma((2, NCH, 2)), dma((2, NCH, 2)),
+            dma((per, n_z)), dma((per, n_z)),
             dma((per,)), dma((per,)),
             dma((2, 3)), dma((2, 3)),
             dma((2, 4, 2)), dma((2, 4, 2)),
@@ -693,7 +702,7 @@
     )(inv, expert_ids.T, route_weights.T, tokens, gate_weight, up_weight, down_weight)
     fresh = fresh.reshape(n_dp, 3, dr, BLK)
 
-    step = max(1, BLK // dr if dr < BLK else 4)
+    step = n_dp // 2
     rows = step * dr
     grid = n_dp // step
     out_w = jax.ShapeDtypeStruct((1, n_dp * dr, BLK), BF16)
@@ -704,6 +713,7 @@
         out_shape=(out_w, out_w, out_w, jax.ShapeDtypeStruct((3, grid, rows // BLK, 1), F32)),
         in_specs=[pl.BlockSpec((step, 3, dr, BLK), lambda i: (i, 0, 0, 0))],
         out_specs=(spec_w, spec_w, spec_w, pl.BlockSpec((3, 1, rows // BLK, 1), lambda i: (0, i, 0, 0))),
+        compiler_params=pltpu.CompilerParams(vmem_limit_bytes=48 * 1024 * 1024),
     )(fresh)
     scales = scales.reshape(3, 1, -1, 1)
 

time: 175 us -> 165 us (0.943)
  Pallas kernels: 170 us -> 158 us
  local copies, waits for them, and re-layouts: 1.3 us -> 3.86 us
    pallas_call x1, Pallas kernels: 162 us -> 155 us  [local(): pl.pallas_call(routed_kernel, out_shape=(jax.ShapeDtypeStruct((NY, NX, 2,...]
    pallas_call x1, Pallas kernels: 8.08 us -> 3.11 us  [local(): pl.pallas_call(quantize_kernel, grid=(grid,), out_shape=(out_w, out_w, ou...]
    unnamed x3 -> x5, local copies, waits for them, and re-layouts: 0.65 us -> 3.2 us
where the time goes in v4:
time: 165 us; the launch traced here: 164 us
  Pallas kernels  158 us (96%)
  local copies, waits for them, and re-layouts  3.86 us (2%)
    pallas_call x1, Pallas kernels, local(): pl.pallas_call(routed_kernel, out_shape=(jax.ShapeDtypeStruct((NY, NX, 2,...  155 us

profile of v4, /device:TPU:10, one launch (start us, length us, event | category | flops | bytes accessed | tf_op | source)
XLA Modules:
  0.0 163.7 jit_solution(10950081762271730955)
XLA Ops:
  0.6 1.3 select_reduce_fusion.inv
  1.9 154.7 %shard_map.110 = (bf16[4,4,2,3,224,128]{5,4,3,2,1,0:T(8,128)(2,1)}, bf16[64,896]{1,0:T(8,128)(2,1)}) custom-call(s32[32]{0:T(128)} %select_reduce_fusion.inv, s32[8,64]{1,0:T(8,128)} %bitcast.5, f32[8,64]{1,0:T(8,128)} %bitcast.6, bf16[64,896]{1,0:T(8,128)(2,1)} %tok.1, bf16[32,224,128]{2,1,0:T(8,128)(2,1)} %wg.1, bf16[32,224,128]{2,1,0:T(8,128)(2,1)} %wu.1, ...), custom_call_target="tpu_custom_call" | custom-call | tf_op jit(solution)/shard_map/pallas_call | solution.py:651
  156.6 0.0 copy-start
  156.7 2.6 %copy-done = bf16[4,4,2,3,224,128]{5,4,3,2,1,0:T(8,128)(2,1)S(1)} copy-done((bf16[4,4,2,3,224,128]{5,4,3,2,1,0:T(8,128)(2,1)S(1)}, bf16[4,4,2,3,224,128]{5,4,3,2,1,0:T(8,128)(2,1)}, u32[]{:S(2)}) %copy-start) | copy-done | bytes 5505048
  159.2 0.0 copy-start.1
  159.2 3.1 %shard_map.111 = (bf16[1,7168,128]{2,1,0:T(8,128)(2,1)}, bf16[1,7168,128]{2,1,0:T(8,128)(2,1)}, bf16[1,7168,128]{2,1,0:T(8,128)(2,1)}, f32[3,2,28,1]{3,2,1,0:T(8,128)S(1)}) custom-call(bf16[32,3,224,128]{3,2,1,0:T(8,128)(2,1)S(1)} %bitcast.4), custom_call_target="tpu_custom_call" | custom-call | tf_op jit(solution)/shard_map/pallas_call | solution.py:710
  162.3 0.1 reduce
  162.4 0.7 reshape.18
  163.1 0.0 copy-done.1
  163.1 0.6 copy.16
Async XLA Ops:
  156.6 2.6 %copy-start = (bf16[4,4,2,3,224,128]{5,4,3,2,1,0:T(8,128)(2,1)S(1)}, bf16[4,4,2,3,224,128]{5,4,3,2,1,0:T(8,128)(2,1)}, u32[]{:S(2)}) copy-start(bf16[4,4,2,3,224,128]{5,4,3,2,1,0:T(8,128)(2,1)} %get-tuple-element.11) | copy-start | bytes 16515076
  159.2 3.9 %copy-start.1 = (bf16[64,896]{1,0:T(8,128)(2,1)S(1)}, bf16[64,896]{1,0:T(8,128)(2,1)}, u32[]{:S(2)}) copy-start(bf16[64,896]{1,0:T(8,128)(2,1)} %get-tuple-element.41) | copy-start | bytes 344068

commit v5 on v4

--- a/solution.py
+++ b/solution.py
@@ -10,7 +10,7 @@
 EPS = 1e-06
 NY, NX = 4, 4
 NCH = 4
-REST = NCH + 4
+REST = NCH + 6
 MESH = pl.DeviceIdType.MESH
 F32, BF16 = jnp.float32, jnp.bfloat16
 
@@ -18,8 +18,8 @@
 def routed_kernel(
     inv, ids, rw, tok, wg, wu, wd,
     fresh, mix,
-    wog, wou, wod, wsg, wsu, wsd, packed, st_a, st_b, tokp, ids_all, pos_all, hots, slot_w, xs, xg, part,
-    hg, hu, rg, ru, qg, qu, r2g, r2u, hid, outp, zb, fin, ob,
+    wog, wou, wod, wsg, wsu, wsd, packed, st_a, st_b, tokp, ids_all, hots, places, row_w, xs, xg, part, dens,
+    hg, hu, rg, ru, r2g, r2u, hid, zb, fin, ob,
     loc, ids_s, ids_r, z_s, z_r, t_s, t_r, w_s, w_r, r0_s, r0_r, r1_s, r1_r, r2_s, r2_r,
     a1_s, a1_r, a2_s, a2_r, a3_s, a3_r, zo_s, zo_r, m_s, m_r, f1_s, f1_r, f2_s, f2_r,
 ):
@@ -37,6 +37,8 @@
     eb = n_e // NCH
     rows_ch = eb * CAP
     slots = n_e * CAP
+    dense = tg * top
+    rows_d = dense // NCH
     dc = 2 * dr
 
     def at(chip):
@@ -197,12 +199,41 @@
     my_w = jnp.zeros((n_e, lanes), F32)
     for i in range(top):
         my_w = jnp.where(mine[i : i + 1, :] == e_iota, rw4[i : i + 1, :], my_w)
+    e_row = lax.broadcasted_iota(jnp.int32, (n_e, n_e), 0)
+    e_col = lax.broadcasted_iota(jnp.int32, (n_e, n_e), 1)
+    below = jnp.where(e_col < e_row, 1.0, 0.0).astype(BF16)
+    d_iota = lax.broadcasted_iota(jnp.int32, (n_e, rows_d), 1).astype(F32)
+    p_dense = lax.broadcasted_iota(jnp.int32, (CAP, rows_d), 0).astype(F32)
+
+    def dense_places(named):
+        count = jnp.broadcast_to(jnp.sum(named, axis=1, keepdims=True), (n_e, rows_d))
+        start = jnp.dot(below, count.astype(BF16), preferred_element_type=F32)
+        out = []
+        for m in range(NCH):
+            at_row = d_iota + float(m * rows_d) - start
+            out.append(jnp.where((at_row >= 0.0) & (at_row < count), at_row, -1.0))
+        return out
+
+    def spots(held):
+        n = held.shape[0]
+        hot = jnp.where(held.reshape(n, 1, rows_d) == p_dense[None], 1.0, 0.0)
+        return hot.reshape(n * CAP, rows_d)
+
+    my_named = jnp.where(my_pos >= 0.0, 1.0, 0.0)
+    my_places = dense_places(my_named)
     p_iota = lax.broadcasted_iota(jnp.int32, (CAP, lanes), 0).astype(F32)
+    slot_w = []
     for q in range(NCH):
         pe = my_pos[q * eb : (q + 1) * eb, :].reshape(eb, 1, lanes)
         we = my_w[q * eb : (q + 1) * eb, :].reshape(eb, 1, lanes)
         ws = jnp.sum(jnp.where(pe == p_iota[None], we, 0.0), axis=2, keepdims=True)
-        slot_w[q * rows_ch : (q + 1) * rows_ch, :] = jnp.broadcast_to(ws.reshape(rows_ch, 1), (rows_ch, BLK))
+        slot_w.append(jnp.broadcast_to(ws.reshape(rows_ch, 1), (rows_ch, BLK)))
+    for m in range(NCH):
+        acc = jnp.zeros((rows_d, BLK), F32)
+        for q in range(max(0, m - 1), min(NCH, m + 2)):
+            hot = spots(my_places[m][q * eb : (q + 1) * eb, :])
+            acc = acc + lax.dot_general(hot, slot_w[q], (((0,), (0,)), ((), ())), preferred_element_type=F32, precision=lax.Precision.HIGHEST)
+        row_w[m * rows_d : (m + 1) * rows_d, :] = acc
 
     far = n_z // 2
     hp = per // 2
@@ -243,14 +274,16 @@
         ids = ids_all[b * NX]
         for i in range(1, NX):
             ids = jnp.maximum(ids, ids_all[b * NX + i])
-        pos_all[b] = positions(ids)
-
-        def hot(q, _):
-            pe = pos_all[b, pl.ds(pl.multiple_of(q * eb, eb), eb), :].reshape(eb, 1, lanes)
+        pos = positions(ids)
+        for i in range(NX):
+            held = dense_places(jnp.where((pos >= 0.0) & (lane_g == i), 1.0, 0.0))
+            for m in range(NCH):
+                places[b * NX + i, m] = held[m]
+
+        for q in range(NCH):
+            pe = pos[q * eb : (q + 1) * eb, :].reshape(eb, 1, lanes)
             hots[b, q] = jnp.where(pe == want[None], 1.0, 0.0).astype(BF16).reshape(eb * NX * CAP, lanes)
-            return 0
-
-        return lax.fori_loop(0, NCH, hot, 0)
+        return 0
 
     for s in range(1, far):
         lax.fori_loop(NY * (s - 1) // (far - 1), NY * s // (far - 1), place, 0)
@@ -265,8 +298,10 @@
 
     def pick(q, b):
         tokens = xs[pl.ds(b * NX, NX)].reshape(lanes, dc)
-        got = jnp.dot(hots[b, q], tokens, preferred_element_type=F32)
-        xg[pl.ds(q * eb, eb), b] = got.astype(BF16).reshape(eb, NX * CAP, dc)
+        he = eb // 2
+        for i in range(2):
+            got = jnp.dot(hots[b, q, pl.ds(i * he * NX * CAP, he * NX * CAP), :], tokens, preferred_element_type=F32)
+            xg[pl.ds(q * eb + i * he, he), b] = got.astype(BF16).reshape(he, NX * CAP, dc)
 
     def by_core(own, other):
         return jnp.concatenate([jnp.where(h == 0, own, other), jnp.where(h == 0, other, own)], axis=0)
@@ -276,8 +311,24 @@
         w = jnp.concatenate([by_core(wog[e], wsg[e]), by_core(wou[e], wsu[e])], axis=1)
         return jnp.dot(a, w, preferred_element_type=F32).reshape(nc, CAP, 2 * BLK)
 
+    def slots_of(q):
+        return pl.ds(pl.multiple_of(q * rows_ch, rows_ch), rows_ch)
+
     def rows_of(q):
-        return pl.ds(pl.multiple_of(q * rows_ch, rows_ch), rows_ch)
+        return pl.ds(pl.multiple_of(q * rows_d, rows_d), rows_d)
+
+    def with_near(q, work):
+        @pl.when(q == 0)
+        def _():
+            work(0, 2)
+
+        @pl.when((q > 0) & (q < NCH - 1))
+        def _():
+            work(q - 1, 3)
+
+        @pl.when(q == NCH - 1)
+        def _():
+            work(NCH - 2, 2)
 
     hy, hx = NY // 2, NX // 2
 
@@ -291,17 +342,17 @@
 
     def r0_copy(q, way, up):
         if up:
-            src, dst = part.at[(y + 2) % NY, pl.ds(way * hx, hx), rows_of(q), pl.ds(BLK, BLK)], hu
+            src, dst = dens.at[(y + 2) % NY, pl.ds(way * hx, hx), rows_of(q), pl.ds(BLK, BLK)], hu
         else:
-            src, dst = part.at[pl.ds(way * hy, hy), (x + 2) % NX, rows_of(q), pl.ds(0, BLK)], hg
+            src, dst = dens.at[pl.ds(way * hy, hy), (x + 2) % NX, rows_of(q), pl.ds(0, BLK)], hg
         u = int(up)
         return remote(src, dst.at[way, :, rows_of(q), :], r0_s.at[u, q, way], r0_r.at[u, q, way], at(chip_near(way, up)))
 
     def r1_copy(q, way, up):
         if up:
-            src, dst = part.at[near(way, up), :, rows_of(q), pl.ds(BLK, BLK)], ru
+            src, dst = dens.at[near(way, up), :, rows_of(q), pl.ds(BLK, BLK)], ru
         else:
-            src, dst = part.at[:, near(way, up), rows_of(q), pl.ds(0, BLK)], rg
+            src, dst = dens.at[:, near(way, up), rows_of(q), pl.ds(0, BLK)], rg
         u = int(up)
         return remote(src, dst.at[way, :, rows_of(q), :], r1_s.at[u, q, way], r1_r.at[u, q, way], at(chip_near(way, up)))
 
@@ -310,13 +361,13 @@
         for way in range(2):
             r0_copy(q, way, False).wait_recv()
             half_y = pl.ds(way * hy, hy)
-            got = part[half_y, near(way, False), rows, pl.ds(0, BLK)].astype(F32) + hg[way, :, rows, :].astype(F32)
-            part[half_y, near(way, False), rows, pl.ds(0, BLK)] = got.astype(BF16)
+            got = dens[half_y, near(way, False), rows, pl.ds(0, BLK)].astype(F32) + hg[way, :, rows, :].astype(F32)
+            dens[half_y, near(way, False), rows, pl.ds(0, BLK)] = got.astype(BF16)
             r1_copy(q, way, False).start()
             r0_copy(q, way, True).wait_recv()
             half_x = pl.ds(way * hx, hx)
-            got = part[near(way, True), half_x, rows, pl.ds(BLK, BLK)].astype(F32) + hu[way, :, rows, :].astype(F32)
-            part[near(way, True), half_x, rows, pl.ds(BLK, BLK)] = got.astype(BF16)
+            got = dens[near(way, True), half_x, rows, pl.ds(BLK, BLK)].astype(F32) + hu[way, :, rows, :].astype(F32)
+            dens[near(way, True), half_x, rows, pl.ds(BLK, BLK)] = got.astype(BF16)
             r1_copy(q, way, True).start()
 
     def first(q):
@@ -330,18 +381,33 @@
             return 0
 
         lax.fori_loop(0, eb // 2, pair, 0)
+    def compact(m):
+        def work(w, n):
+            experts = pl.ds(pl.multiple_of(w * eb, eb), n * eb)
+            near_slots = pl.ds(pl.multiple_of(w * rows_ch, rows_ch), n * rows_ch)
+
+            def one(b, _):
+                got = []
+                for i in range(NX):
+                    hot = spots(places[b * NX + i, m, experts, :]).astype(BF16)
+                    got.append(lax.dot_general(hot, part[b, i, near_slots, :], (((0,), (0,)), ((), ())), preferred_element_type=F32))
+                for i in range(NX):
+                    dens[b, i, rows_of(m), :] = got[i].astype(BF16)
+                return 0
+
+            lax.fori_loop(0, NY, one, 0)
+
+        with_near(m, work)
         for way in range(2):
-            r0_copy(q, way, False).start()
-            r0_copy(q, way, True).start()
-
-        return 0
+            r0_copy(m, way, False).start()
+            r0_copy(m, way, True).start()
 
     def r2_copy(q, k, up):
         if up:
             to = (x + k) % NX
-            return remote(qu.at[to, rows_of(q), :], r2u.at[k - 1, rows_of(q), :], r2_s.at[1, q, k - 1], r2_r.at[1, q, k - 1], at(y * NX + to))
+            return remote(dens.at[y, to, rows_of(q), pl.ds(BLK, BLK)], r2u.at[k - 1, rows_of(q), :], r2_s.at[1, q, k - 1], r2_r.at[1, q, k - 1], at(y * NX + to))
         to = (y + k) % NY
-        return remote(qg.at[to, rows_of(q), :], r2g.at[k - 1, rows_of(q), :], r2_s.at[0, q, k - 1], r2_r.at[0, q, k - 1], at(to * NX + x))
+        return remote(dens.at[to, x, rows_of(q), pl.ds(0, BLK)], r2g.at[k - 1, rows_of(q), :], r2_s.at[0, q, k - 1], r2_r.at[0, q, k - 1], at(to * NX + x))
 
     def second(q):
         rows = rows_of(q)
@@ -349,10 +415,10 @@
             r1_copy(q, way, False).wait_recv()
 
         def sum_g(i, _):
-            t = part[i, x, rows, pl.ds(0, BLK)].astype(F32)
+            t = dens[i, x, rows, pl.ds(0, BLK)].astype(F32)
             for way in range(2):
                 t = t + rg[way, i, rows, :].astype(F32)
-            qg[i, rows, :] = t.astype(BF16)
+            dens[i, x, rows, pl.ds(0, BLK)] = t.astype(BF16)
             return 0
 
         lax.fori_loop(0, NY, sum_g, 0)
@@ -362,10 +428,10 @@
             r1_copy(q, way, True).wait_recv()
 
         def sum_u(i, _):
-            t = part[y, i, rows, pl.ds(BLK, BLK)].astype(F32)
+            t = dens[y, i, rows, pl.ds(BLK, BLK)].astype(F32)
             for way in range(2):
                 t = t + ru[way, i, rows, :].astype(F32)
-            qu[i, rows, :] = t.astype(BF16)
+            dens[y, i, rows, pl.ds(BLK, BLK)] = t.astype(BF16)
             return 0
 
         lax.fori_loop(0, NX, sum_u, 0)
@@ -379,10 +445,10 @@
             return y * NX + (x + k) % NX
         return ((y + k) % NY) * NX + x
 
-    hr_ch = rows_ch // 2
+    hr_ch = rows_d // 2
 
     def half_of(q, along_x, part_of=None):
-        start, size = q * rows_ch + (0 if along_x else hr_ch), hr_ch
+        start, size = q * rows_d + (0 if along_x else hr_ch), hr_ch
         if part_of is not None:
             start, size = start + part_of * (hr_ch // 2), hr_ch // 2
         return pl.ds(pl.multiple_of(start, hr_ch // 2), size)
@@ -427,13 +493,13 @@
             r2_copy(q, k, False).wait_recv()
         for k in range(1, NX):
             r2_copy(q, k, True).wait_recv()
-        gate = qg[y, rows, :].astype(F32)
+        gate = dens[y, x, rows, pl.ds(0, BLK)].astype(F32)
         for k in range(NY - 1):
             gate = gate + r2g[k, rows, :].astype(F32)
-        up = qu[x, rows, :].astype(F32)
+        up = dens[y, x, rows, pl.ds(BLK, BLK)].astype(F32)
         for k in range(NX - 1):
             up = up + r2u[k, rows, :].astype(F32)
-        value = gate / (1.0 + jnp.exp(-gate)) * up * slot_w[rows, :]
+        value = gate / (1.0 + jnp.exp(-gate)) * up * row_w[rows, :]
         hid[y, x, rows, :] = value.astype(BF16)
         for k in range(1, NX):
             a1_copy(q, k, True).start()
@@ -453,14 +519,33 @@
                 a2_from(q, way, along_x).wait_recv()
                 a3_copy(q, way, along_x).start()
 
-    def down(q):
+    def arrive(q):
         for along_x in (True, False):
             for way in range(2):
                 a3_from(q, way, along_x).wait_recv()
 
+    def down(q):
+        experts = pl.ds(pl.multiple_of(q * eb, eb), eb)
+
+        def work(w, n):
+            near_rows = pl.ds(pl.multiple_of(w * rows_d, rows_d), n * rows_d)
+
+            def one(b, _):
+                got = []
+                for i in range(NX):
+                    hot = jnp.concatenate([spots(places[b * NX + i, w + d, experts, :]) for d in range(n)], axis=1).astype(BF16)
+                    got.append(jnp.dot(hot, hid[b, i, near_rows, :], preferred_element_type=F32))
+                for i in range(NX):
+                    part[b, i, slots_of(q), pl.ds(0, BLK)] = got[i].astype(BF16)
+                return 0
+
+            lax.fori_loop(0, NY, one, 0)
+
+        with_near(q, work)
+
         def pair(i, _):
             e = q * eb + 2 * i
-            both = hid[:, :, pl.ds(pl.multiple_of(e * CAP, 2 * CAP), 2 * CAP), :].astype(F32).reshape(nc, 2 * CAP, BLK)
+            both = part[:, :, pl.ds(pl.multiple_of(e * CAP, 2 * CAP), 2 * CAP), pl.ds(0, BLK)].astype(F32).reshape(nc, 2 * CAP, BLK)
             for o in range(2):
                 a = both[:, o * CAP : (o + 1) * CAP, :].reshape(nc * CAP, BLK).astype(BF16)
                 w = by_core(wod[e + o], wsd[e + o])
@@ -470,10 +555,10 @@
 
         lax.fori_loop(0, eb // 2, pair, 0)
 
-    stages = [first]
+    stages = [first, compact]
     stages += [pass_on, second]
     stages += [third]
-    stages += [spread, forward, down]
+    stages += [spread, forward, arrive, down]
 
     def beat(t, _):
         for n, stage in enumerate(stages):
@@ -497,6 +582,11 @@
         return 0
 
     lax.fori_loop(0, NCH + len(stages) - 1, beat, 0)
+    for s in range(far):
+        for way in range(2):
+            z_copy(s, way).wait_send()
+    outp = xs
+
     per_row = NX // per
 
     def zo_copy(to, n):
@@ -579,9 +669,6 @@
         return 0
 
     lax.fori_loop(1, n_z, z_done, 0)
-    for s in range(far):
-        for way in range(2):
-            z_copy(s, way).wait_send()
     for i in range(per):
 
         @pl.when(per * j + i != c)
@@ -663,22 +750,20 @@
             vm((NY, NX, 2, 3, dr // 2, BLK), BF16),
             vm((per, tg, dc), BF16),
             vm((nc, top, lanes), jnp.int32),
-            vm((NY, n_e, lanes), F32),
             vm((NY, NCH, slots // NCH * NX, lanes), BF16),
-            vm((slots, BLK), F32),
+            vm((nc, NCH, n_e, tg * top // NCH), F32),
+            vm((tg * top, BLK), F32),
             vm((nc, tg, dc), BF16),
             vm((n_e, NY, NX * CAP, dc), BF16),
             vm((NY, NX, slots, 2 * BLK), BF16),
-            vm((2, NY // 2, slots, BLK), BF16),
-            vm((2, NX // 2, slots, BLK), BF16),
-            vm((2, NY, slots, BLK), BF16),
-            vm((2, NX, slots, BLK), BF16),
-            vm((NY, slots, BLK), BF16),
-            vm((NX, slots, BLK), BF16),
-            vm((NY - 1, slots, BLK), BF16),
-            vm((NX - 1, slots, BLK), BF16),
-            vm((NY, NX, slots, BLK), BF16),
-            vm((nc, tg, dc), BF16),
+            vm((NY, NX, tg * top, 2 * BLK), BF16),
+            vm((2, NY // 2, tg * top, BLK), BF16),
+            vm((2, NX // 2, tg * top, BLK), BF16),
+            vm((2, NY, tg * top, BLK), BF16),
+            vm((2, NX, tg * top, BLK), BF16),
+            vm((NY - 1, tg * top, BLK), BF16),
+            vm((NX - 1, tg * top, BLK), BF16),
+            vm((NY, NX, tg * top, BLK), BF16),
             vm((per, n_z, tg, dc), BF16),
             vm((per, tg, dc), BF16),
             vm((per, tg, dc), BF16),
@@ -698,7 +783,7 @@
             dma((2, 3)), dma((2, 3)),
             dma((2, 4, 2)), dma((2, 4, 2)),
         ],
-        compiler_params=pltpu.CompilerParams(collective_id=0, has_side_effects=True, vmem_limit_bytes=62 * 1024 * 1024),
+        compiler_params=pltpu.CompilerParams(collective_id=0, has_side_effects=True, vmem_limit_bytes=63 * 1024 * 1024),
     )(inv, expert_ids.T, route_weights.T, tokens, gate_weight, up_weight, down_weight)
     fresh = fresh.reshape(n_dp, 3, dr, BLK)
 

time: 165 us -> 154 us (0.933)
  Pallas kernels: 158 us -> 148 us
    pallas_call x1, Pallas kernels: 155 us -> 145 us  [local(): pl.pallas_call(routed_kernel, out_shape=(jax.ShapeDtypeStruct((NY, NX, 2,...]
where the time goes in v5:
time: 154 us
  Pallas kernels  148 us (96%)
  local copies, waits for them, and re-layouts  3.86 us (3%)
    pallas_call x1, Pallas kernels, local(): pl.pallas_call(routed_kernel, out_shape=(jax.ShapeDtypeStruct((NY, NX, 2,...  145 us
    unnamed x5, local copies, waits for them, and re-layouts  3.2 us
    pallas_call x1, Pallas kernels, local(): pl.pallas_call(quantize_kernel, grid=(grid,), out_shape=(out_w, out_w, ou...  3.11 us

profile of v5, /device:TPU:10, one launch (start us, length us, event | category | flops | bytes accessed | tf_op | source)
XLA Modules:
  0.0 154.2 jit_solution(11895852601349262368)
XLA Ops:
  0.6 1.3 select_reduce_fusion.inv
  1.9 145.2 %shard_map.110 = (bf16[4,4,2,3,224,128]{5,4,3,2,1,0:T(8,128)(2,1)}, bf16[64,896]{1,0:T(8,128)(2,1)}) custom-call(s32[32]{0:T(128)} %select_reduce_fusion.inv, s32[8,64]{1,0:T(8,128)} %bitcast.5, f32[8,64]{1,0:T(8,128)} %bitcast.6, bf16[64,896]{1,0:T(8,128)(2,1)} %tok.1, bf16[32,224,128]{2,1,0:T(8,128)(2,1)} %wg.1, bf16[32,224,128]{2,1,0:T(8,128)(2,1)} %wu.1, ...), custom_call_target="tpu_custom_call" | custom-call | tf_op jit(solution)/shard_map/pallas_call | solution.py:738
  147.1 0.0 copy-start
  147.1 2.6 %copy-done = bf16[4,4,2,3,224,128]{5,4,3,2,1,0:T(8,128)(2,1)S(1)} copy-done((bf16[4,4,2,3,224,128]{5,4,3,2,1,0:T(8,128)(2,1)S(1)}, bf16[4,4,2,3,224,128]{5,4,3,2,1,0:T(8,128)(2,1)}, u32[]{:S(2)}) %copy-start) | copy-done | bytes 5505048
  149.7 0.0 copy-start.1
  149.7 3.1 %shard_map.111 = (bf16[1,7168,128]{2,1,0:T(8,128)(2,1)}, bf16[1,7168,128]{2,1,0:T(8,128)(2,1)}, bf16[1,7168,128]{2,1,0:T(8,128)(2,1)}, f32[3,2,28,1]{3,2,1,0:T(8,128)S(1)}) custom-call(bf16[32,3,224,128]{3,2,1,0:T(8,128)(2,1)S(1)} %bitcast.4), custom_call_target="tpu_custom_call" | custom-call | tf_op jit(solution)/shard_map/pallas_call | solution.py:795
  152.8 0.1 reduce
  152.9 0.7 reshape.18
  153.6 0.0 copy-done.1
  153.6 0.6 copy.16
Async XLA Ops:
  147.1 2.6 %copy-start = (bf16[4,4,2,3,224,128]{5,4,3,2,1,0:T(8,128)(2,1)S(1)}, bf16[4,4,2,3,224,128]{5,4,3,2,1,0:T(8,128)(2,1)}, u32[]{:S(2)}) copy-start(bf16[4,4,2,3,224,128]{5,4,3,2,1,0:T(8,128)(2,1)} %get-tuple-element.11) | copy-start | bytes 16515076
  149.7 3.9 %copy-start.1 = (bf16[64,896]{1,0:T(8,128)(2,1)S(1)}, bf16[64,896]{1,0:T(8,128)(2,1)}, u32[]{:S(2)}) copy-start(bf16[64,896]{1,0:T(8,128)(2,1)} %get-tuple-element.41) | copy-start | bytes 344068

commit v6 on v5

--- a/solution.py
+++ b/solution.py
@@ -16,9 +16,9 @@
 
 
 def routed_kernel(
-    inv, ids, rw, tok, wg, wu, wd,
+    placement, ids, rw, tok, wg, wu, wd,
     fresh, mix,
-    wog, wou, wod, wsg, wsu, wsd, packed, st_a, st_b, tokp, ids_all, hots, places, row_w, xs, xg, part, dens,
+    inv, wog, wou, wod, wsg, wsu, wsd, packed, st_a, st_b, tokp, ids_all, hots, places, row_w, xs, xg, part, dens,
     hg, hu, rg, ru, r2g, r2u, hid, zb, fin, ob,
     loc, ids_s, ids_r, z_s, z_r, t_s, t_r, w_s, w_r, r0_s, r0_r, r1_s, r1_r, r2_s, r2_r,
     a1_s, a1_r, a2_s, a2_r, a3_s, a3_r, zo_s, zo_r, m_s, m_r, f1_s, f1_r, f2_s, f2_r,
@@ -76,6 +76,14 @@
         def _():
             pl.semaphore_signal(barrier, inc=1, device_id={"dp": 2 * (per * j + i) + h, "mp": home}, device_id_type=MESH)
 
+    def find(s, _):
+        e = jnp.int32(0)
+        for i in range(n_e):
+            e = jnp.maximum(e, jnp.where(placement[i] == s, jnp.int32(i), jnp.int32(0)))
+        inv[s] = e
+        return 0
+
+    lax.fori_loop(0, n_e, find, 0)
     for cp in own_w:
         cp.wait()
 
@@ -577,7 +585,11 @@
                 f1_from(k, True).wait_recv()
             for cp in f2_own:
                 cp.start()
-            f2_start(range(max(NX, NY)))
+            f2_start((0, 2))
+
+        @pl.when(t == REST + 1)
+        def _():
+            f2_start((1, 3))
 
         return 0
 
@@ -727,8 +739,6 @@
     dc, per, lanes = 2 * dr, wide // (2 * dr), NX * tg
     slots = n_e * CAP
 
-    order = jnp.arange(n_e, dtype=jnp.int32)
-    inv = jnp.sum(jnp.where(placement_of[:, None] == order[None, :], order[:, None], 0), axis=0)
 
     vm = pltpu.VMEM
     dma = pltpu.SemaphoreType.DMA
@@ -743,7 +753,8 @@
         ),
         in_specs=[pl.BlockSpec(memory_space=pltpu.SMEM), vmem, vmem, vmem, hbm, hbm, hbm],
         out_specs=(hbm, vmem),
-        scratch_shapes=weights
+        scratch_shapes=[pltpu.SMEM((n_e,), jnp.int32)]
+        + weights
         + [
             vm((NY, NX, 2, 3, dr, BLK), BF16),
             vm((NX, NY, 2, 3, dr // 2, BLK), BF16),
@@ -784,7 +795,7 @@
             dma((2, 4, 2)), dma((2, 4, 2)),
         ],
         compiler_params=pltpu.CompilerParams(collective_id=0, has_side_effects=True, vmem_limit_bytes=63 * 1024 * 1024),
-    )(inv, expert_ids.T, route_weights.T, tokens, gate_weight, up_weight, down_weight)
+    )(placement_of, expert_ids.T, route_weights.T, tokens, gate_weight, up_weight, down_weight)
     fresh = fresh.reshape(n_dp, 3, dr, BLK)
 
     step = n_dp // 2

time: 154 us -> 153 us (level)
  no operation moved by 1% of the time
where the time goes in v6:
time: 153 us
  Pallas kernels  149 us (97%)
  local copies, waits for them, and re-layouts  3.86 us (3%)
    pallas_call x1, Pallas kernels, local(): pl.pallas_call(routed_kernel, out_shape=(jax.ShapeDtypeStruct((NY, NX, 2,...  145 us
    unnamed x5, local copies, waits for them, and re-layouts  3.2 us
    pallas_call x1, Pallas kernels, local(): pl.pallas_call(quantize_kernel, grid=(grid,), out_shape=(out_w, out_w, ou...  3.11 us

profile of v6, /device:TPU:10, one launch (start us, length us, event | category | flops | bytes accessed | tf_op | source)
XLA Modules:
  0.0 153.1 jit_solution(4482095603287895403)
XLA Ops:
  0.6 145.4 %shard_map.110 = (bf16[4,4,2,3,224,128]{5,4,3,2,1,0:T(8,128)(2,1)}, bf16[64,896]{1,0:T(8,128)(2,1)}) custom-call(s32[32]{0:T(128)} %placement.1, s32[8,64]{1,0:T(8,128)} %bitcast.5, f32[8,64]{1,0:T(8,128)} %bitcast.6, bf16[64,896]{1,0:T(8,128)(2,1)} %tok.1, bf16[32,224,128]{2,1,0:T(8,128)(2,1)} %wg.1, bf16[32,224,128]{2,1,0:T(8,128)(2,1)} %wu.1, ...), custom_call_target="tpu_custom_call" | custom-call | tf_op jit(solution)/shard_map/pallas_call | solution.py:748
  146.1 0.0 copy-start
  146.1 2.6 %copy-done = bf16[4,4,2,3,224,128]{5,4,3,2,1,0:T(8,128)(2,1)S(1)} copy-done((bf16[4,4,2,3,224,128]{5,4,3,2,1,0:T(8,128)(2,1)S(1)}, bf16[4,4,2,3,224,128]{5,4,3,2,1,0:T(8,128)(2,1)}, u32[]{:S(2)}) %copy-start) | copy-done | bytes 5505048
  148.6 0.0 copy-start.1
  148.6 3.1 %shard_map.111 = (bf16[1,7168,128]{2,1,0:T(8,128)(2,1)}, bf16[1,7168,128]{2,1,0:T(8,128)(2,1)}, bf16[1,7168,128]{2,1,0:T(8,128)(2,1)}, f32[3,2,28,1]{3,2,1,0:T(8,128)S(1)}) custom-call(bf16[32,3,224,128]{3,2,1,0:T(8,128)(2,1)S(1)} %bitcast.4), custom_call_target="tpu_custom_call" | custom-call | tf_op jit(solution)/shard_map/pallas_call | solution.py:806
  151.7 0.1 reduce
  151.8 0.7 reshape.17
  152.5 0.0 copy-done.1
  152.5 0.6 copy.15
Async XLA Ops:
  146.1 2.6 %copy-start = (bf16[4,4,2,3,224,128]{5,4,3,2,1,0:T(8,128)(2,1)S(1)}, bf16[4,4,2,3,224,128]{5,4,3,2,1,0:T(8,128)(2,1)}, u32[]{:S(2)}) copy-start(bf16[4,4,2,3,224,128]{5,4,3,2,1,0:T(8,128)(2,1)} %get-tuple-element.11) | copy-start | bytes 16515076
  148.6 3.9 %copy-start.1 = (bf16[64,896]{1,0:T(8,128)(2,1)S(1)}, bf16[64,896]{1,0:T(8,128)(2,1)}, u32[]{:S(2)}) copy-start(bf16[64,896]{1,0:T(8,128)(2,1)} %get-tuple-element.36) | copy-start | bytes 344068
